TPU v7x, 768 devices: a whole 4x8x12 slice. The times are simulated.
768 devices in a mesh: blk: 96 (over x, y_lo, z), dp: 8 (over y_hi, core).
Axes of the slice: x: 4, y: 8 (y_hi: 4, y_lo: 2; y = y_hi * 2 + y_lo), z: 12, core: 2. Of those that a mesh axis runs over, the one named last changes fastest.
Arguments:
- image_emb: bfloat16 [196608, 1152], P(('blk', 'dp')), may hold values from -0.1875 to 0.1875
- text_feat: bfloat16 [196608, 1152], P(('blk', 'dp')), may hold values from -0.1875 to 0.1875
- text_proj: bfloat16 [1152, 1152], P('dp'), may hold values from -0.1875 to 0.1875
- pos_index: int32 [768, 256], P(('blk', 'dp')), may hold values from 0 to 255, each once within a row
- scale: float32 [1], replicated, may hold values from 4 to 8
- bias: float32 [1], replicated, may hold values from -2 to 0
Outputs:
- grad_image: float32 [196608, 1152], P(('blk', 'dp'))
- grad_text_feat: float32 [196608, 1152], P(('blk', 'dp'))
- grad_proj: float32 [1152, 1152], P('dp')
Inputs may be any that keep to these rules, and one draw needn't show every extreme that they name: Each row of pos_index is a permutation of 0 to 255.
All inputs are finite; a program needn't handle non-finite values.
Results may differ from a plain program's by a relative error of at most 0.0053.
Values may be sent and summed in bfloat16 or wider, within the bound.
A program may use at most 64 MiB of HBM per device.

v0:
```python
import jax
import jax.numpy as jnp
from jax import lax
from jax.sharding import PartitionSpec as P


def from_behind(block, axis, distance):
    devices = range(lax.axis_size(axis))
    route = [((i - distance) % len(devices), i) for i in devices]
    return lax.ppermute(block, axis, route)


def row_norm(values):
    return jnp.sqrt(jnp.sum(values * values, axis=-1, keepdims=True) + 1e-06)


def norm_back(values, norms, grads):
    inner = jnp.sum(values * grads, axis=-1, keepdims=True)
    return grads / norms - values * inner / (norms * norms * norms)


def pair_dot(left, right):
    return lax.dot_general(
        left, right, (((1,), (1,)), ((), ())), preferred_element_type=jnp.float32
    )


def lead_dot(left, right):
    return lax.dot_general(
        left, right, (((0,), (0,)), ((), ())), preferred_element_type=jnp.float32
    )


def local(image_emb, text_feat, text_proj, pos_index, scale, bias):
    rows = image_emb.shape[0]
    full_proj = lax.all_gather(text_proj, "dp", axis=0, tiled=True)
    text_emb = jnp.dot(text_feat, full_proj, preferred_element_type=jnp.float32)
    image_f = image_emb.astype(jnp.float32)
    image_norm = row_norm(image_f)
    text_norm = row_norm(text_emb)
    image_unit = (image_f / image_norm).astype(jnp.bfloat16)
    text_unit = (text_emb / text_norm).astype(jnp.bfloat16)
    prev_unit = from_behind(text_unit, "blk", 1)
    factor = scale[0]
    offset = bias[0]
    own_logit = factor * pair_dot(image_unit, text_unit) + offset
    near_logit = factor * pair_dot(image_unit, prev_unit) + offset
    columns = lax.broadcasted_iota(jnp.int32, (rows, rows), 1)
    label = jnp.where(columns == pos_index[0][:, None], 1.0, -1.0).astype(jnp.float32)
    own_coef = (-label * jax.nn.sigmoid(-label * own_logit)).astype(jnp.bfloat16)
    near_coef = jax.nn.sigmoid(near_logit).astype(jnp.bfloat16)
    grad_iu = factor * jnp.dot(
        own_coef, text_unit, preferred_element_type=jnp.float32
    ) + factor * jnp.dot(near_coef, prev_unit, preferred_element_type=jnp.float32)
    own_text = factor * lead_dot(own_coef, image_unit)
    near_text = factor * lead_dot(near_coef, image_unit)
    from_next = from_behind(near_text, "blk", -1)
    grad_tu = own_text + from_next
    grad_image = norm_back(image_f, image_norm, grad_iu)
    grad_te = norm_back(text_emb, text_norm, grad_tu).astype(jnp.bfloat16)
    grad_text_feat = pair_dot(grad_te, full_proj)
    group_sum = lax.psum_scatter(
        lead_dot(text_feat, grad_te), "dp", scatter_dimension=0, tiled=True
    )
    grad_proj = lax.psum(group_sum, "blk")
    return (grad_image, grad_text_feat, grad_proj)


def solution(mesh):
    return jax.shard_map(
        local,
        mesh=mesh,
        in_specs=(
            P(("blk", "dp"), None),
            P(("blk", "dp"), None),
            P("dp", None),
            P(("blk", "dp"), None),
            P(),
            P(),
        ),
        out_specs=(P(("blk", "dp"), None), P(("blk", "dp"), None), P("dp", None)),
        check_vma=False,
    )
```

profile of v0, /device:TPU:16, one launch (start us, length us, event | category | flops | bytes accessed | tf_op | source)
XLA Modules:
  0.0 1078.2 jit_solution(16952043740724070826)
XLA Ops:
  7.2 0.7 all-gather.2.cloned.1.call-update
  8.0 54.5 %all-gather.2.cloned.1.call-done = bf16[1152,1152]{1,0:T(8,128)(2,1)} async-done(((bf16[144,1152]{1,0:T(8,128)(2,1)}), bf16[1152,1152]{1,0:T(8,128)(2,1)}) %all-gather.2.cloned.1.call-update) | async-done | bytes 2654224 | tf_op jit(solution)/shard_map/all_gather | solution.py:36
  62.5 2.8 multiply_reduce_fusion.1
  65.5 3.6 collective-permute-start
  70.6 16.6 %collective-permute-done = bf16[256,1152]{1,0:T(8,128)(2,1)S(1)} collective-permute-done((bf16[256,1152]{1,0:T(8,128)(2,1)S(1)}, bf16[256,1152]{1,0:T(8,128)(2,1)S(1)}, u32[]{:S(2)}, u32[]{:S(2)}) %collective-permute-start) | collective-permute-done | bytes 589856 | tf_op jit(solution)/shard_map/ppermute | solution.py:10
  87.2 0.4 fusion.20
  87.6 0.4 copy-done.2
  88.0 0.4 convolution_multiply_fusion
  88.6 3.6 collective-permute-start.1
  92.3 0.5 fusion.19
  92.7 25.1 %collective-permute-done.1 = f32[256,1152]{1,0:T(8,128)S(1)} collective-permute-done((f32[256,1152]{1,0:T(8,128)S(1)}, f32[256,1152]{1,0:T(8,128)S(1)}, u32[]{:S(2)}, u32[]{:S(2)}) %collective-permute-start.1) | collective-permute-done | bytes 1179680 | tf_op jit(solution)/shard_map/ppermute | solution.py:10
  117.9 0.5 multiply_reduce_fusion
  118.7 3.4 convolution_bitcast_fusion
  122.1 6.9 copy.11
  129.0 0.3 fusion.25
  129.4 0.7 copy-done.3
  130.1 0.5 fusion.4
  130.5 64.8 %reduce-scatter.4.cloned.1.call-done = f32[144,1152]{1,0:T(8,128)} async-done(((f32[1152,1152]{1,0:T(8,128)}), f32[144,1152]{1,0:T(8,128)}) %reduce-scatter.4.cloned.1.call-update) | async-done | bytes 663568
  195.4 2.5 copy.12
  197.9 1.3 fusion.6
  199.2 0.9 copy-done.6
  200.1 2.1 fusion.26
  202.1 867.1 %all-reduce.2.cloned.1.call-done = f32[144,1152]{0,1:T(8,128)} async-done(((f32[144,1152]{0,1:T(8,128)}), f32[144,1152]{0,1:T(8,128)}) %all-reduce.2.cloned.1.call-update) | async-done | bytes 663568 | tf_op jit(solution)/shard_map/psum | solution.py:65
  1069.3 2.4 copy.10
  (23 shorter events, 1.1 us)
Async XLA Ops:
  7.2 55.3 %copy-start = (bf16[256,1152]{1,0:T(8,128)(2,1)S(1)}, bf16[256,1152]{1,0:T(8,128)(2,1)}, u32[]{:S(2)}) copy-start(bf16[256,1152]{1,0:T(8,128)(2,1)} %param.7) | copy-start | bytes 1769476
  7.2 55.3 %all-gather.2.cloned.1.call-start = ((), (), s32[]{:S(2)}) async-start(), calls=%async_computation.1 | async-start | bytes 2985984 | tf_op jit(solution)/shard_map/all_gather | solution.py:36
  7.9 187.5 %reduce-scatter.4.cloned.1.call-start = ((), (), s32[]{:S(2)}) async-start(), calls=%async_computation.3 | async-start | bytes 5971968
  65.3 5.0 copy-start.1
  65.5 21.7 %collective-permute-start = (bf16[256,1152]{1,0:T(8,128)(2,1)S(1)}, bf16[256,1152]{1,0:T(8,128)(2,1)S(1)}, u32[]{:S(2)}, u32[]{:S(2)}) collective-permute-start(bf16[256,1152]{1,0:T(8,128)(2,1)S(1)} %divide_convert_fusion), channel_id=1, source_target_pairs={{760,0},{0,8},{8,16},{16,24},{24,32},{32,40},{40,48},{48,56},{56,6... | collective-permute-start | bytes 1769480 | tf_op jit(solution)/shard_map/ppermute | solution.py:10
  87.2 0.8 copy-start.2
  88.0 0.7 copy-start.4
  88.0 4.3 copy-start.7
  88.6 29.3 %collective-permute-start.1 = (f32[256,1152]{1,0:T(8,128)S(1)}, f32[256,1152]{1,0:T(8,128)S(1)}, u32[]{:S(2)}, u32[]{:S(2)}) collective-permute-start(f32[256,1152]{1,0:T(8,128)S(1)} %convolution_multiply_fusion), channel_id=1, source_target_pairs={{8,0},{16,8},{24,16},{32,24},{40,32},{48,40},{56,48},{64,56},{72,6... | collective-permute-start | bytes 3538952 | tf_op jit(solution)/shard_map/ppermute | solution.py:10
  128.9 940.3 %all-reduce.2.cloned.1.call-start = ((), (), s32[]{:S(2)}) async-start(), calls=%async_computation.2 | async-start | bytes 2359296 | tf_op jit(solution)/shard_map/psum | solution.py:65
  129.0 1.1 copy-start.3
  129.0 1.1 copy-start.5
  197.9 2.2 copy-start.6
Sparse Core Ops, SparseCore 0:
  10.4 52.0 all-gather.1
  129.1 66.2 reduce-scatter.3
  198.6 870.6 all-reduce.1
where the time goes:
time: 1080 us
  waiting for transfers between devices  1030 us (95%)
  between operations  15.2 us (1%)
  local copies, waits for them, and re-layouts  14 us (1%)
  matrix products  10.9 us (1%)
    psum x1, waiting for transfers between devices, local(): grad_proj = lax.psum(group_sum, 'blk')  867 us
    unnamed x4, waiting for transfers between devices  65.5 us
    all_gather x1, waiting for transfers between devices, local(): full_proj = lax.all_gather(text_proj, 'dp', axis=0, tiled=True)  54.5 us
    ppermute x2, waiting for transfers between devices, from_behind(): return lax.ppermute(block, axis, route)  41.7 us
  transfers between devices with their start and end apart: 5, of which 5 were waited for; matrix products, arithmetic and copies ran while one was open for 0% of the time, Pallas kernels for 0%

commit v1 on v0

v1 whole, which is shorter than its diff:
```python
import jax
import jax.numpy as jnp
from jax import lax
from jax.experimental import pallas as pl
from jax.experimental.pallas import tpu as pltpu
from jax.sharding import PartitionSpec as P

MESH = pl.DeviceIdType.MESH
BF = jnp.bfloat16
F32 = jnp.float32
NX, NY, NZ, NH = 4, 8, 12, 4
ROWS, D, SH = 256, 1152, 144
PART = 32
UA, UB = 7, 4
UN = UA + UB
TILES = 81
COLS = 384
IMG = 2


def place():
    b, d = lax.axis_index("blk"), lax.axis_index("dp")
    x = b // (2 * NZ)
    low = lax.rem(b // NZ, 2)
    z = lax.rem(b, NZ)
    return b, d, x, (d // 2) * 2 + low, z, lax.rem(d, 2)


def device(x, y, z, c):
    return (x * (2 * NZ) + lax.rem(y, 2) * NZ + z, (y // 2) * 2 + c)


def nt_dot(a, b):
    return lax.dot_general(a, b, (((1,), (1,)), ((), ())), preferred_element_type=F32)


def nn_dot(a, b):
    return jnp.dot(a, b, preferred_element_type=F32)


def sigmoid(v):
    return 1.0 / (1.0 + jnp.exp(-v))


def inv_norm(v):
    return lax.rsqrt(jnp.sum(v * v, axis=-1, keepdims=True) + 1e-06)


def unit_rows(src, unit, inv, step=64):
    def body(i, _):
        rows = pl.ds(pl.multiple_of(i * step, step), step)
        v = src[rows].astype(F32)
        r = inv_norm(v)
        unit[rows] = (v * r).astype(BF)
        if inv is not None:
            inv[rows] = r
        return 0

    lax.fori_loop(0, src.shape[0] // step, body, 0)


def norm_back(src, inv, grad, out, step=64):
    def body(i, _):
        rows = pl.ds(pl.multiple_of(i * step, step), step)
        v, r, g = src[rows].astype(F32), inv[rows], grad[rows]
        inner = jnp.sum(v * g, axis=-1, keepdims=True)
        out[rows] = (r * (g - v * (inner * r * r))).astype(out.dtype)
        return 0

    lax.fori_loop(0, src.shape[0] // step, body, 0)


def by_columns(fn):
    def body(i, _):
        fn(pl.ds(pl.multiple_of(i * COLS, COLS), COLS))
        return 0

    lax.fori_loop(0, D // COLS, body, 0)


def kernel(
    image, feat, proj, pos, scale, bias,
    g_image, g_feat, g_proj,
    full, image_n, feat_p, tft, tft_o, unit_i, unit_n, unit_t, unit_p, inv_i, inv_t, inv_p,
    text, text_p, acc_t, acc_i, gte, gte_o, part, send_a, send_b, got_a, got_b,
    mid_a, mid_b, got_a2, got_b2, zin, got_z, fin,
    s_img, r_img, s_txt, r_txt, s_py, r_py, s_pt, r_pt, s_px, r_px, s_pc, r_pc,
    s_tf, r_tf, s_ge, r_ge, s_a, r_a, s_b, r_b, s_a2, r_a2, s_b2, r_b2,
    s_z, r_z, s_gz, r_gz, s_gx, r_gx, s_gy, r_gy,
):
    b, d, x, y, z, c = place()
    n_blk = lax.axis_size("blk")
    h, low = y // 2, lax.rem(y, 2)
    prev = (lax.rem(b + n_blk - 1, n_blk), d)
    nxt = (lax.rem(b + 1, n_blk), d)
    mate = device(x, y, z, 1 - c)
    xs = [lax.rem(x + o, NX) for o in range(NX)]
    ys = [lax.rem(y + o, NY) for o in range(NY)]
    zs = [lax.rem(z + o, NZ) for o in range(NZ)]
    to_x = [device(v, y, z, c) for v in xs]
    to_y = [device(x, v, z, c) for v in ys]
    to_z = [device(x, y, v, c) for v in zs]
    pending = []

    def send(src, dst, s, r, dev):
        cp = pltpu.make_async_remote_copy(
            src_ref=src, dst_ref=dst, send_sem=s, recv_sem=r, device_id=dev, device_id_type=MESH
        )
        cp.start()
        pending.append(cp)
        return cp

    barrier = pltpu.get_barrier_semaphore()
    partners = to_x[1:] + to_y[1:] + to_z[1:] + [mate, prev, nxt]
    for dev in partners:
        pl.semaphore_signal(barrier, inc=1, device_id=dev, device_id_type=MESH)
    pl.semaphore_wait(barrier, len(partners))

    step = ROWS // IMG
    c_img = [
        send(image.at[pl.ds(i * step, step)], image_n.at[pl.ds(i * step, step)], s_img.at[i], r_img.at[i], prev)
        for i in range(IMG)
    ]
    sign = 2 * low - 1
    mine = pl.multiple_of(d * SH, 16)
    xrow = pl.multiple_of(x * PART, 16)
    c_py, c_pt = [], []
    for k in range(3):
        dev = device(x, lax.rem(y + sign * (k + 1) + NY, NY), z, c)
        c_py.append(
            send(
                proj.at[pl.ds(xrow, PART)],
                full.at[pl.ds(pl.multiple_of(mine + xrow, 16), PART)],
                s_py.at[k], r_py.at[k], dev,
            )
        )
    for k in range(3):
        dev = device(x, lax.rem(y + sign * (k + 1) + NY, NY), z, c)
        c_pt.append(
            send(
                proj.at[pl.ds(NX * PART, SH - NX * PART)],
                full.at[pl.ds(pl.multiple_of(mine + NX * PART, 16), SH - NX * PART)],
                s_pt.at[k], r_pt.at[k], dev,
            )
        )
    c_pc = [send(proj, full.at[pl.ds(mine, SH)], s_pc.at[3], r_pc.at[3], mate)]
    c_txt = send(feat, feat_p, s_txt.at[0], r_txt.at[0], nxt)
    full[pl.ds(mine, SH)] = proj[...]

    for i in range(8):
        pass
    turned = feat[...].T
    for i in range(8):
        tft[i // 2, i % 2] = turned[i * SH : (i + 1) * SH]
    c_tf = send(tft.at[:, 1 - c], tft_o, s_tf.at[0], r_tf.at[0], mate)
    unit_rows(image, unit_i, inv_i)

    rows_of = []
    for k, hop in enumerate((1, -2, 3)):
        src_y = lax.rem(y + sign * hop + NY, NY)
        rows_of.append(((src_y // 2) * 2 + c) * SH)
    c_px = []
    for k in range(3):
        c_py[k].wait_recv()
        where = full.at[pl.ds(pl.multiple_of(rows_of[k] + xrow, 16), PART)]
        c_px.append([send(where, where, s_px.at[k, o - 1], r_px.at[k, o - 1], to_x[o]) for o in range(1, NX)])
    for k in range(3):
        c_pt[k].wait_recv()
        for cp in c_px[k]:
            cp.wait_recv()
        where = full.at[pl.ds(pl.multiple_of(rows_of[k], 16), SH)]
        c_pc.append(send(where, where, s_pc.at[k], r_pc.at[k], mate))
    for cp in c_pc:
        cp.wait_recv()

    def text_cols(cols):
        text[:, cols] = nn_dot(feat[...], full[:, cols])

    by_columns(text_cols)
    unit_rows(text, unit_t, inv_t)
    factor = scale[0]
    offset = bias[0]

    logit = factor * nt_dot(unit_t[...], unit_i[...]) + offset
    hit = lax.broadcasted_iota(jnp.int32, (ROWS, ROWS), 0) == pos[...]
    label = jnp.where(hit, 1.0, -1.0).astype(F32)
    coef = -label * sigmoid(-label * logit)
    coef_t = coef.astype(BF)
    coef_i = coef.T.astype(BF)

    def own_cols(cols):
        acc_t[:, cols] = nn_dot(coef_t, unit_i[:, cols])
        acc_i[:, cols] = nn_dot(coef_i, unit_t[:, cols])

    by_columns(own_cols)

    for i in range(IMG):
        c_img[i].wait_recv()
        rows = pl.ds(i * step, step)
        unit_rows(image_n.at[rows], unit_n.at[rows], None)
        near = sigmoid(factor * nt_dot(unit_t[...], unit_n[rows]) + offset).astype(BF)

        def near_cols(cols):
            acc_t[:, cols] += nn_dot(near, unit_n[rows, cols])

        by_columns(near_cols)

    def scaled(i, _):
        rows = pl.ds(pl.multiple_of(i * 64, 64), 64)
        acc_t[rows] = factor * acc_t[rows]
        return 0

    lax.fori_loop(0, ROWS // 64, scaled, 0)
    norm_back(text, inv_t, acc_t, gte)
    c_ge = send(gte, gte_o, s_ge.at[0], r_ge.at[0], mate)

    def first_half(i, _):
        part[i] = nn_dot(tft[i, c], gte[...])
        return 0

    lax.fori_loop(0, NH, first_half, 0)
    c_tf.wait_recv()
    c_ge.wait_recv()

    def second_half(i, _):
        both = (part[i] + nn_dot(tft_o[i], gte_o[...])).astype(BF)
        for t in range(2 * NX * UN):
            l, xo, u = t // (NX * UN), (t // UN) % NX, t % UN
            if t < TILES:
                row, col = (t // 9) * 16, (t % 9) * 128
                tile = both[row : row + 16, col : col + 128]
            else:
                tile = jnp.zeros((16, 128), BF)
            if u < UA:
                send_a[xo, 2 * i + l, u] = tile
            else:
                send_b[2 * i + l, xo, u - UA] = tile
        return 0

    lax.fori_loop(0, NH, second_half, 0)
    c_a = [send(send_a.at[xs[o]], got_a.at[o - 1], s_a.at[o - 1], r_a.at[o - 1], to_x[o]) for o in range(1, NX)]
    c_b = [send(send_b.at[ys[o]], got_b.at[o - 1], s_b.at[o - 1], r_b.at[o - 1], to_y[o]) for o in range(1, NY)]

    def feat_cols(i, _):
        rows = pl.ds(pl.multiple_of(i * 64, 64), 64)
        g_feat[rows] = nt_dot(gte[rows], full[...]).astype(BF)
        return 0

    lax.fori_loop(0, ROWS // 64, feat_cols, 0)
    c_txt.wait_recv()

    def text_p_cols(cols):
        text_p[:, cols] = nn_dot(feat_p[...], full[:, cols])

    by_columns(text_p_cols)
    unit_rows(text_p, unit_p, None)
    near_p = sigmoid(factor * nt_dot(unit_i[...], unit_p[...]) + offset).astype(BF)

    def image_cols(cols):
        acc_i[:, cols] = factor * (acc_i[:, cols] + nn_dot(near_p, unit_p[:, cols]))

    by_columns(image_cols)
    norm_back(image, inv_i, acc_i, g_image)

    for cp in c_a:
        cp.wait_recv()

    def sum_a(i, _):
        v = send_a[x, i].astype(F32)
        for o in range(NX - 1):
            v = v + got_a[o, i].astype(F32)
        mid_a[i] = v.astype(BF)
        return 0

    lax.fori_loop(0, NY, sum_a, 0)
    c_a2 = [send(mid_a.at[ys[o]], got_a2.at[o - 1], s_a2.at[o - 1], r_a2.at[o - 1], to_y[o]) for o in range(1, NY)]
    for cp in c_b:
        cp.wait_recv()

    def sum_b(i, _):
        v = send_b[y, i].astype(F32)
        for o in range(NY - 1):
            v = v + got_b[o, i].astype(F32)
        mid_b[i] = v.astype(BF)
        return 0

    lax.fori_loop(0, NX, sum_b, 0)
    c_b2 = [send(mid_b.at[xs[o]], got_b2.at[o - 1], s_b2.at[o - 1], r_b2.at[o - 1], to_x[o]) for o in range(1, NX)]
    for cp in c_a2:
        cp.wait_recv()
    v = mid_a[y].astype(F32)
    for o in range(NY - 1):
        v = v + got_a2[o].astype(F32)
    zin[0:UA] = v.astype(BF)
    for cp in c_b2:
        cp.wait_recv()
    v = mid_b[x].astype(F32)
    for o in range(NX - 1):
        v = v + got_b2[o].astype(F32)
    zin[UA:UN] = v.astype(BF)
    zin[UN] = jnp.zeros((16, 128), BF)

    c_z = [send(zin.at[zs[o]], got_z.at[o - 1], s_z.at[o - 1], r_z.at[o - 1], to_z[o]) for o in range(1, NZ)]
    v = zin[z].astype(F32)
    for o in range(NZ - 1):
        c_z[o].wait_recv()
        v = v + got_z[o].astype(F32)
    fin[low, x, z] = v.astype(BF)
    own = fin.at[low, x, z]
    c_gz = [send(own, own, s_gz.at[o - 1], r_gz.at[o - 1], to_z[o]) for o in range(1, NZ)]
    for cp in c_gz:
        cp.wait_recv()
    own = fin.at[low, x]
    c_gx = [send(own, own, s_gx.at[o - 1], r_gx.at[o - 1], to_x[o]) for o in range(1, NX)]
    for cp in c_gx:
        cp.wait_recv()
    own = fin.at[low]
    c_gy = send(own, own, s_gy.at[0], r_gy.at[0], device(x, h * 2 + 1 - low, z, c))
    c_gy.wait_recv()
    for t in range(TILES):
        l, xo, u = t // (NX * UN), (t // UN) % NX, t % UN
        row, col = (t // 9) * 16, (t % 9) * 128
        g_proj[row : row + 16, col : col + 128] = fin[l, xo, u]
    for cp in pending:
        cp.wait_send()


def local(image_emb, text_feat, text_proj, pos_index, scale, bias):
    dma = lambda *shape: [pltpu.SemaphoreType.DMA(shape), pltpu.SemaphoreType.DMA(shape)]
    vm = pltpu.VMEM
    scratch = [
        vm((D, D), BF), vm((ROWS, D), BF), vm((ROWS, D), BF),
        vm((NH, 2, SH, ROWS), BF), vm((NH, SH, ROWS), BF),
        vm((ROWS, D), BF), vm((ROWS, D), BF), vm((ROWS, D), BF), vm((ROWS, D), BF),
        vm((ROWS, 1), F32), vm((ROWS, 1), F32), vm((ROWS, 1), F32),
        vm((ROWS, D), F32), vm((ROWS, D), F32), vm((ROWS, D), F32), vm((ROWS, D), F32),
        vm((ROWS, D), BF), vm((ROWS, D), BF), vm((NH, SH, D), F32),
        vm((NX, NY, UA, 16, 128), BF), vm((NY, NX, UB, 16, 128), BF),
        vm((NX - 1, NY, UA, 16, 128), BF), vm((NY - 1, NX, UB, 16, 128), BF),
        vm((NY, UA, 16, 128), BF), vm((NX, UB, 16, 128), BF),
        vm((NY - 1, UA, 16, 128), BF), vm((NX - 1, UB, 16, 128), BF),
        vm((NZ, 16, 128), BF), vm((NZ - 1, 16, 128), BF), vm((2, NX, NZ, 16, 128), BF),
    ]
    sems = (
        dma(IMG) + dma(1) + dma(3) + dma(3) + dma(3, NX - 1) + dma(4) + dma(1) + dma(1)
        + dma(NX - 1) + dma(NY - 1) + dma(NY - 1) + dma(NX - 1)
        + dma(NZ - 1) + dma(NZ - 1) + dma(NX - 1) + dma(1)
    )
    whole = pl.BlockSpec(memory_space=pltpu.VMEM)
    scalar = pl.BlockSpec(memory_space=pltpu.SMEM)
    g_image, g_feat, g_proj = pl.pallas_call(
        kernel,
        out_shape=(
            jax.ShapeDtypeStruct((ROWS, D), BF),
            jax.ShapeDtypeStruct((ROWS, D), BF),
            jax.ShapeDtypeStruct((SH, D), BF),
        ),
        in_specs=[whole, whole, whole, whole, scalar, scalar],
        out_specs=(whole, whole, whole),
        scratch_shapes=scratch + sems,
        compiler_params=pltpu.CompilerParams(
            collective_id=0, has_side_effects=True, vmem_limit_bytes=44 * 1024 * 1024
        ),
        name="contrast_back",
    )(image_emb, text_feat, text_proj, pos_index, scale, bias)
    return g_image.astype(F32), g_feat.astype(F32), g_proj.astype(F32)


def solution(mesh):
    return jax.shard_map(
        local,
        mesh=mesh,
        in_specs=(
            P(("blk", "dp"), None),
            P(("blk", "dp"), None),
            P("dp", None),
            P(("blk", "dp"), None),
            P(),
            P(),
        ),
        out_specs=(P(("blk", "dp"), None), P(("blk", "dp"), None), P("dp", None)),
        check_vma=False,
    )
```

time: 1080 us -> 105 us (0.10)
  the two profiles are of different devices: /device:TPU:16 before, /device:TPU:8 now
where the time goes in v1:
time: 105 us; the launch traced here: 104 us
  Pallas kernels  95.6 us (91%)
  local copies, waits for them, and re-layouts  3.77 us (4%)
  other arithmetic  3.06 us (3%)
  between operations  1.94 us (2%)
    pallas_call x1, Pallas kernels, local(): pl.pallas_call(kernel, out_shape=(jax.ShapeDtypeStruct((ROWS, D), BF), ja...  95.6 us
    unnamed x8, local copies, waits for them, and re-layouts  3.77 us
    convert_element_type x3, other arithmetic, local(): return (g_image.astype(F32), g_feat.astype(F32), g_proj.astype(F32))  3.06 us

profile of v1, /device:TPU:8, one launch (start us, length us, event | category | flops | bytes accessed | tf_op | source)
XLA Modules:
  0.0 104.4 jit_solution(2035345235185079305)
XLA Ops:
  1.9 0.0 copy-start
  1.9 1.1 %copy-done = bf16[256,1152]{1,0:T(8,128)(2,1)S(1)} copy-done((bf16[256,1152]{1,0:T(8,128)(2,1)S(1)}, bf16[256,1152]{1,0:T(8,128)(2,1)}, u32[]{:S(2)}) %copy-start) | copy-done | bytes 589848
  3.0 0.0 copy-start.1
  3.0 1.1 %copy-done.1 = bf16[256,1152]{1,0:T(8,128)(2,1)S(1)} copy-done((bf16[256,1152]{1,0:T(8,128)(2,1)S(1)}, bf16[256,1152]{1,0:T(8,128)(2,1)}, u32[]{:S(2)}) %copy-start.1) | copy-done | bytes 589848
  4.1 0.0 copy-start.2
  4.1 1.0 copy-done.2
  5.0 0.0 copy-start.3
  5.0 0.7 copy-done.3
  5.7 95.6 %contrast_back.1 = (bf16[256,1152]{1,0:T(8,128)(2,1)S(1)}, bf16[256,1152]{1,0:T(8,128)(2,1)S(1)}, bf16[144,1152]{1,0:T(8,128)(2,1)S(1)}) custom-call(bf16[256,1152]{1,0:T(8,128)(2,1)S(1)} %copy-done, bf16[256,1152]{1,0:T(8,128)(2,1)S(1)} %copy-done.1, bf16[144,1152]{1,0:T(8,128)(2,1)S(1)} %copy-done.2, s32[1,256]{1,0:T(1,128)S(1)} %copy-done.3, ...), custom_call_target="tpu_custom_call" | custom-call | tf_op jit(solution)/shard_map/contrast_back/pallas_call | solution.py:351
  101.4 1.1 %convert_element_type.10 = f32[256,1152]{1,0:T(8,128)} convert(bf16[256,1152]{1,0:T(8,128)(2,1)S(1)} %get-tuple-element.7) | non-fusion elementwise | flops 294912 | bytes 1769472 | tf_op jit(solution)/shard_map/convert_element_type | solution.py:366
  102.4 1.1 %convert_element_type.9 = f32[256,1152]{1,0:T(8,128)} convert(bf16[256,1152]{1,0:T(8,128)(2,1)S(1)} %get-tuple-element.6) | non-fusion elementwise | flops 294912 | bytes 1769472 | tf_op jit(solution)/shard_map/convert_element_type | solution.py:366
  103.5 0.9 convert_element_type.11
Async XLA Ops:
  1.9 1.1 %copy-start = (bf16[256,1152]{1,0:T(8,128)(2,1)S(1)}, bf16[256,1152]{1,0:T(8,128)(2,1)}, u32[]{:S(2)}) copy-start(bf16[256,1152]{1,0:T(8,128)(2,1)} %image.1) | copy-start | bytes 1769476
  3.0 1.1 %copy-start.1 = (bf16[256,1152]{1,0:T(8,128)(2,1)S(1)}, bf16[256,1152]{1,0:T(8,128)(2,1)}, u32[]{:S(2)}) copy-start(bf16[256,1152]{1,0:T(8,128)(2,1)} %feat.1) | copy-start | bytes 1769476
  4.1 1.0 copy-start.2
  5.0 0.7 copy-start.3

commit v2 on v1

v2 whole, which is shorter than its diff:
```python
import jax
import jax.numpy as jnp
from jax import lax
from jax.experimental import pallas as pl
from jax.experimental.pallas import tpu as pltpu
from jax.sharding import PartitionSpec as P

MESH = pl.DeviceIdType.MESH
BF = jnp.bfloat16
F32 = jnp.float32
NX, NY, NZ, NH = 4, 8, 12, 4
ROWS, D, SH = 256, 1152, 144
PART = 32
UA, UB = 8, 3
UN = UA + UB
TILES = 81
COLS = 384
IMG = 4
VIA = 2


def place():
    b, d = lax.axis_index("blk"), lax.axis_index("dp")
    x = b // (2 * NZ)
    low = lax.rem(b // NZ, 2)
    z = lax.rem(b, NZ)
    return b, d, x, (d // 2) * 2 + low, z, lax.rem(d, 2)


def device(x, y, z, c):
    return (x * (2 * NZ) + lax.rem(y, 2) * NZ + z, (y // 2) * 2 + c)


def nt_dot(a, b):
    return lax.dot_general(a, b, (((1,), (1,)), ((), ())), preferred_element_type=F32)


def nn_dot(a, b):
    return jnp.dot(a, b, preferred_element_type=F32)


def sigmoid(v):
    return 1.0 / (1.0 + jnp.exp(-v))


def inv_norm(v):
    return lax.rsqrt(jnp.sum(v * v, axis=-1, keepdims=True) + 1e-06)


def unit_rows(src, unit, inv, step=64):
    def body(i, _):
        rows = pl.ds(pl.multiple_of(i * step, step), step)
        v = src[rows].astype(F32)
        r = inv_norm(v)
        unit[rows] = (v * r).astype(BF)
        if inv is not None:
            inv[rows] = r
        return 0

    lax.fori_loop(0, src.shape[0] // step, body, 0)


def norm_back(src, inv, grad, factor, out, step, done=None):
    for i in range(src.shape[0] // step):
        rows = pl.ds(i * step, step)
        v, r, g = src[rows].astype(F32), inv[rows], factor * grad[rows]
        inner = jnp.sum(v * g, axis=-1, keepdims=True)
        out[rows] = (r * (g - v * (inner * r * r))).astype(out.dtype)
        if done is not None:
            done(i, rows)


def by_columns(fn):
    def body(i, _):
        fn(pl.ds(pl.multiple_of(i * COLS, COLS), COLS))
        return 0

    lax.fori_loop(0, D // COLS, body, 0)


def kernel(
    image_h, feat_h, proj_h, pos_h, scale, bias,
    g_image, g_feat, g_proj,
    full, image, feat, pos, image_n, feat_p, feat_k, tft, tft_o, unit_in, unit_tp, inv_i, inv_t,
    text, text_p, acc_t, acc_i, coef_o, gte, gte_o, part, send_a, send_b, got_a, got_b,
    mid_a, mid_b, got_a2, got_b2, zin, got_z, fin,
    hop, s_in, relay, s_fwd, r_hop,
    s_img, r_img, s_txt, r_txt, s_py, r_py, s_pt, r_pt, s_px, r_px, s_pc, r_pc,
    s_tf, r_tf, s_ge, r_ge, s_a, r_a, s_b, r_b, s_a2, r_a2, s_b2, r_b2,
    s_z, r_z, s_gz, r_gz, s_gx, r_gx, s_gy, r_gy,
):
    b, d, x, y, z, c = place()
    n_blk = lax.axis_size("blk")
    h, low = y // 2, lax.rem(y, 2)
    prev = (lax.rem(b + n_blk - 1, n_blk), d)
    nxt = (lax.rem(b + 1, n_blk), d)
    mate = device(x, y, z, 1 - c)
    xs = [lax.rem(x + o, NX) for o in range(NX)]
    ys = [lax.rem(y + o, NY) for o in range(NY)]
    zs = [lax.rem(z + o, NZ) for o in range(NZ)]
    to_x = [device(v, y, z, c) for v in xs]
    to_y = [device(x, v, z, c) for v in ys]
    to_z = [device(x, y, v, c) for v in zs]
    pending = []
    col = x * 2 + low
    before, after = lax.rem(col + 7, 8), lax.rem(col + 1, 8)
    to_before = device(before // 2, 2 * h + lax.rem(before, 2), z, c)
    to_after = device(after // 2, 2 * h + lax.rem(after, 2), z, c)

    def copy(src, dst, s, r, dev):
        return pltpu.make_async_remote_copy(
            src_ref=src, dst_ref=dst, send_sem=s, recv_sem=r, device_id=dev, device_id_type=MESH
        )

    def send(src, dst, s, r, dev):
        cp = copy(src, dst, s, r, dev)
        cp.start()
        pending.append(cp)
        return cp

    def rows16(start, size):
        return pl.ds(pl.multiple_of(start, 16), size)

    barrier = pltpu.get_barrier_semaphore()
    partners = to_x[1:] + to_y[1:] + [mate, prev, nxt, to_z[1], to_z[NZ - 1], to_before, to_after]
    for dev in partners:
        pl.semaphore_signal(barrier, inc=1, device_id=dev, device_id_type=MESH)
    mine = d * SH
    loads = [
        pltpu.make_async_copy(a, to, s_in.at[i])
        for i, (a, to) in enumerate(
            ((image_h, image), (feat_h, feat), (proj_h, full.at[rows16(mine, SH)]), (pos_h, pos))
        )
    ]
    for cp in loads:
        cp.start()
    pl.semaphore_wait(barrier, len(partners))

    def pass_on(i):
        if i:
            pl.semaphore_wait(relay.at[i - 1], 2)
        if i < 5:
            for dev in (to_z[1], to_z[NZ - 1]):
                pl.semaphore_signal(relay.at[i], inc=1, device_id=dev, device_id_type=MESH)

    step = ROWS // IMG
    direct = IMG - VIA
    cut = lambda ref, i: ref.at[pl.ds(i * step, step)]
    c_img = [copy(cut(image_h, i), cut(image_n, i), s_img.at[i], r_img.at[i], prev) for i in range(IMG)]
    c_hop = [
        copy(cut(image_h, direct + i), cut(hop, i), s_img.at[direct + i], r_hop.at[i], to_before) for i in range(VIA)
    ]
    c_fwd = [
        copy(cut(hop, i), cut(image_n, direct + i), s_fwd.at[i], r_img.at[direct + i], to_z[NZ - 1])
        for i in range(VIA)
    ]
    c_txt = copy(feat_h, feat_p, s_txt.at[0], r_txt.at[0], nxt)
    pending += c_img + [c_txt]
    for i in range(direct):
        c_img[i].start()

    @pl.when(z == 0)
    def _():
        for i in range(VIA):
            c_hop[i].start()

    @pl.when(z != 0)
    def _():
        for i in range(VIA):
            c_img[direct + i].start()

    sign = 2 * low - 1
    xrow = x * PART
    rest = SH - NX * PART
    c_py, c_pt = [], []
    ahead = [device(x, lax.rem(y + sign * (k + 1) + NY, NY), z, c) for k in range(3)]
    for k in range(3):
        c_py.append(
            send(
                proj_h.at[rows16(xrow, PART)], full.at[rows16(mine + xrow, PART)],
                s_py.at[k], r_py.at[k], ahead[k],
            )
        )
    c_pc = [[], [], [], [send(proj_h, full.at[rows16(mine, SH)], s_pc.at[15], r_pc.at[15], mate)]]
    for k in range(3):
        c_pt.append(
            send(
                proj_h.at[pl.ds(NX * PART, rest)], full.at[rows16(mine + NX * PART, rest)],
                s_pt.at[k], r_pt.at[k], ahead[k],
            )
        )

    @pl.when(z != NZ - 1)
    def _():
        c_txt.start()

    for cp in loads:
        cp.wait()
    turned = feat[...].T
    for i in range(8):
        tft[i % 2, i // 2] = turned[i * SH : (i + 1) * SH]
    c_tf = send(tft.at[1 - c], tft_o, s_tf.at[0], r_tf.at[0], mate)
    unit_rows(image, unit_in.at[pl.ds(0, ROWS)], inv_i)
    for i in range(NH):
        feat_k[i] = feat[:, i * 2 * SH : (i + 1) * 2 * SH]

    pairs, rows_of = [], []
    for hop in (1, -2, 3):
        src_y = lax.rem(y + sign * hop + NY, NY)
        pairs.append(src_y // 2)
        rows_of.append(((src_y // 2) * 2 + c) * SH)

    def to_mate(k, i, start, size):
        where = full.at[rows16(start, size)]
        c_pc[k].append(send(where, where, s_pc.at[k * 5 + i], r_pc.at[k * 5 + i], mate))

    c_px = []
    for k in range(3):
        c_py[k].wait_recv()
        where = full.at[rows16(rows_of[k] + xrow, PART)]
        c_px.append([send(where, where, s_px.at[k, o - 1], r_px.at[k, o - 1], to_x[o]) for o in range(1, NX)])
        to_mate(k, 0, rows_of[k] + xrow, PART)

    @pl.when(z == 0)
    def _():
        for i in range(VIA):
            c_hop[i].wait_recv()
            c_fwd[i].start()

    def add_text(pair, first):
        rhs_rows = rows16(pair * (2 * SH), 2 * SH)

        def cols_of(cols):
            v = nn_dot(feat_k[pair], full[rhs_rows, cols])
            text[:, cols] = v if first else text[:, cols] + v

        by_columns(cols_of)

    c_pc[3][0].wait_recv()
    add_text(h, True)
    for k in range(3):
        for o in range(1, NX):
            c_px[k][o - 1].wait_recv()
            to_mate(k, o, rows_of[k] + lax.rem(x + NX - o, NX) * PART, PART)
        c_pt[k].wait_recv()
        to_mate(k, 4, rows_of[k] + NX * PART, rest)
        if k:
            for cp in c_pc[k - 1]:
                cp.wait_recv()
            add_text(pairs[k - 1], False)

    @pl.when(z == NZ - 1)
    def _():
        c_txt.start()

    for i in range(IMG):
        c_img[i].wait_recv()
        unit_rows(image_n.at[pl.ds(i * step, step)], unit_in.at[pl.ds(ROWS + i * step, step)], None)
    for cp in c_pc[2]:
        cp.wait_recv()
    add_text(pairs[2], False)
    unit_t = unit_tp.at[pl.ds(0, ROWS)]
    unit_rows(text, unit_t, inv_t)
    factor = scale[0]
    offset = bias[0]

    logit = factor * nt_dot(unit_t[...], unit_in[...]) + offset
    hit = lax.broadcasted_iota(jnp.int32, (ROWS, ROWS), 0) == pos[...]
    label = jnp.where(hit, 1.0, -1.0).astype(F32)
    coef = (-label * sigmoid(-label * logit[:, :ROWS])).astype(BF)
    coef_o[...] = coef
    coef_all = jnp.concatenate([coef, sigmoid(logit[:, ROWS:]).astype(BF)], axis=1)

    def text_grads(cols):
        acc_t[:, cols] = nn_dot(coef_all, unit_in[:, cols])

    by_columns(text_grads)
    c_ge = []

    def share(i, rows):
        c_ge.append(send(gte.at[rows], gte_o.at[rows], s_ge.at[i], r_ge.at[i], mate))

    norm_back(text, inv_t, acc_t, factor, gte, 64, share)
    pass_on(0)
    tft_c = tft[c].reshape(NH * SH, ROWS)

    def first_half(cols):
        part[:, cols] = nn_dot(tft_c, gte[:, cols])

    by_columns(first_half)
    pass_on(1)
    c_tf.wait_recv()
    for cp in c_ge:
        cp.wait_recv()

    def group(i):
        return lax.rem(h + 1 + i, NH)

    def second_half(i):
        hh = group(i)
        both = (part[rows16(hh * SH, SH)] + nn_dot(tft_o[hh], gte_o[...])).astype(BF)
        for t in range(2 * NX * UN):
            l, xo, u = t // (NX * UN), (t // UN) % NX, t % UN
            if t < TILES:
                row, col = (t // 9) * 16, (t % 9) * 128
                tile = both[row : row + 16, col : col + 128]
            else:
                tile = jnp.zeros((16, 128), BF)
            if u < UA:
                send_a[xo, 2 * hh + l, u] = tile
            else:
                send_b[2 * hh + l, xo, u - UA] = tile

    def a_copy(i, o):
        two = pl.ds(2 * group(i), 2)
        return copy(send_a.at[xs[o], two], got_a.at[o - 1, two], s_a.at[o - 1, i], r_a.at[o - 1, i], to_x[o])

    def b_copy(to):
        return copy(send_b.at[to], got_b.at[y], s_b.at[to], r_b.at[y], device(x, to, z, c))

    def a2_copy(to):
        return copy(mid_a.at[to], got_a2.at[y], s_a2.at[to], r_a2.at[y], device(x, to, z, c))

    def start_group(i, _):
        second_half(i)
        for o in range(1, NX):
            a_copy(i, o).start()
        for l in range(2):
            b_copy(2 * group(i) + l).start()
        return 0

    twin = 2 * h + 1 - low
    lax.fori_loop(0, NH - 1, start_group, 0)
    second_half(NH - 1)
    for o in range(1, NX):
        a_copy(NH - 1, o).start()
    b_copy(twin).start()
    pass_on(2)

    def feat_cols(i, _):
        cols = pl.ds(pl.multiple_of(i * COLS, COLS), COLS)
        g_feat[:, cols] = nt_dot(gte[...], full[cols]).astype(BF)
        return 0

    lax.fori_loop(0, D // COLS, feat_cols, 0)

    def sum_a(i):
        for o in range(1, NX):
            a_copy(i, o).wait_recv()
        for l in range(2):
            at = 2 * group(i) + l
            v = send_a[x, at].astype(F32)
            for o in range(NX - 1):
                v = v + got_a[o, at].astype(F32)
            mid_a[at] = v.astype(BF)

    def a_group(i, _):
        sum_a(i)
        for l in range(2):
            a2_copy(2 * group(i) + l).start()
        return 0

    pass_on(3)
    lax.fori_loop(0, NH - 1, a_group, 0)
    sum_a(NH - 1)
    a2_copy(twin).start()
    pass_on(4)

    def received(sem, slots, at):
        copy(slots.at[at], slots.at[at], sem.at[at], sem.at[at], mate).wait_recv()

    for o in range(1, NY):
        received(r_b, got_b, ys[o])

    def sum_b(i, _):
        v = send_b[y, i].astype(F32)
        for o in range(1, NY):
            v = v + got_b[ys[o], i].astype(F32)
        mid_b[i] = v.astype(BF)
        return 0

    lax.fori_loop(0, NX, sum_b, 0)
    c_b2 = [send(mid_b.at[xs[o]], got_b2.at[o - 1], s_b2.at[o - 1], r_b2.at[o - 1], to_x[o]) for o in range(1, NX)]

    for o in range(1, NY):
        received(r_a2, got_a2, ys[o])
    v = mid_a[y].astype(F32)
    for o in range(1, NY):
        v = v + got_a2[ys[o]].astype(F32)
    zin[0:UA] = v.astype(BF)
    for cp in c_b2:
        cp.wait_recv()
    v = mid_b[x].astype(F32)
    for o in range(NX - 1):
        v = v + got_b2[o].astype(F32)
    zin[UA:UN] = v.astype(BF)
    zin[UN] = jnp.zeros((16, 128), BF)

    pass_on(5)
    c_z = [send(zin.at[zs[o]], got_z.at[o - 1], s_z.at[o - 1], r_z.at[o - 1], to_z[o]) for o in range(1, NZ)]
    v = zin[z].astype(F32)
    for o in range(NZ - 1):
        c_z[o].wait_recv()
        v = v + got_z[o].astype(F32)
    fin[low, x, z] = v.astype(BF)
    own = fin.at[low, x, z]
    c_gz = [send(own, own, s_gz.at[o - 1], r_gz.at[o - 1], to_z[o]) for o in range(1, NZ)]

    c_txt.wait_recv()

    def text_p_cols(cols):
        text_p[:, cols] = nn_dot(feat_p[...], full[:, cols])

    by_columns(text_p_cols)
    unit_rows(text_p, unit_tp.at[pl.ds(ROWS, ROWS)], None)
    near_p = sigmoid(factor * nt_dot(unit_in[:ROWS], unit_tp[ROWS:]) + offset).astype(BF)
    coef_both = jnp.concatenate([coef_o[...].T, near_p], axis=1)

    def image_cols(cols):
        acc_i[:, cols] = nn_dot(coef_both, unit_tp[:, cols])

    by_columns(image_cols)
    norm_back(image, inv_i, acc_i, factor, g_image, 64)

    for cp in c_gz:
        cp.wait_recv()
    own = fin.at[low, x, pl.ds(0, UN)]
    c_gy = [send(own, own, s_gy.at[0], r_gy.at[0], device(x, twin, z, c))]
    c_gx = [send(own, own, s_gx.at[o - 1], r_gx.at[o - 1], to_x[o]) for o in range(1, NX)]
    for o in (1, 3, 2):
        c_gx[o - 1].wait_recv()
        got = fin.at[low, xs[NX - o], pl.ds(0, UN)]
        c_gy.append(send(got, got, s_gy.at[o], r_gy.at[o], device(x, twin, z, c)))
    for cp in c_gy:
        cp.wait_recv()
    for t in range(TILES):
        l, xo, u = t // (NX * UN), (t // UN) % NX, t % UN
        row, col = (t // 9) * 16, (t % 9) * 128
        g_proj[row : row + 16, col : col + 128] = fin[l, xo, u]
    for cp in pending:
        cp.wait_send()
    for i in range(NH):
        for o in range(1, NX):
            a_copy(i, o).wait_send()
    for o in range(1, NY):
        b_copy(ys[o]).wait_send()
        a2_copy(ys[o]).wait_send()

    @pl.when(z == 0)
    def _():
        for cp in c_fwd:
            cp.wait_send()


def local(image_emb, text_feat, text_proj, pos_index, scale, bias):
    dma = lambda *shape: [pltpu.SemaphoreType.DMA(shape), pltpu.SemaphoreType.DMA(shape)]
    vm = pltpu.VMEM
    scratch = [
        vm((D, D), BF), vm((ROWS, D), BF), vm((ROWS, D), BF), vm((1, ROWS), jnp.int32),
        vm((ROWS, D), BF), vm((ROWS, D), BF), vm((NH, ROWS, 2 * SH), BF),
        vm((2, NH, SH, ROWS), BF), vm((NH, SH, ROWS), BF),
        vm((2 * ROWS, D), BF), vm((2 * ROWS, D), BF),
        vm((ROWS, 1), F32), vm((ROWS, 1), F32),
        vm((ROWS, D), F32), vm((ROWS, D), F32), vm((ROWS, D), F32), vm((ROWS, D), F32),
        vm((ROWS, ROWS), BF), vm((ROWS, D), BF), vm((ROWS, D), BF), vm((NH * SH, D), F32),
        vm((NX, NY, UA, 16, 128), BF), vm((NY, NX, UB, 16, 128), BF),
        vm((NX - 1, NY, UA, 16, 128), BF), vm((NY, NX, UB, 16, 128), BF),
        vm((NY, UA, 16, 128), BF), vm((NX, UB, 16, 128), BF),
        vm((NY, UA, 16, 128), BF), vm((NX - 1, UB, 16, 128), BF),
        vm((NZ, 16, 128), BF), vm((NZ - 1, 16, 128), BF), vm((2, NX, NZ, 16, 128), BF),
        vm((VIA * ROWS // IMG, D), BF), pltpu.SemaphoreType.DMA((4,)), pltpu.SemaphoreType.REGULAR((5,)),
        pltpu.SemaphoreType.DMA((VIA,)), pltpu.SemaphoreType.DMA((VIA,)),
    ]
    sems = (
        dma(IMG) + dma(1) + dma(3) + dma(3) + dma(3, NX - 1) + dma(16) + dma(1) + dma(4)
        + dma(NX - 1, NH) + dma(NY) + dma(NY) + dma(NX - 1)
        + dma(NZ - 1) + dma(NZ - 1) + dma(NX - 1) + dma(NX)
    )
    whole = pl.BlockSpec(memory_space=pltpu.VMEM)
    scalar = pl.BlockSpec(memory_space=pltpu.SMEM)
    far = pl.BlockSpec(memory_space=pltpu.HBM)
    g_image, g_feat, g_proj = pl.pallas_call(
        kernel,
        out_shape=(
            jax.ShapeDtypeStruct((ROWS, D), BF),
            jax.ShapeDtypeStruct((ROWS, D), BF),
            jax.ShapeDtypeStruct((SH, D), BF),
        ),
        in_specs=[far, far, far, far, scalar, scalar],
        out_specs=(whole, whole, whole),
        scratch_shapes=scratch + sems,
        compiler_params=pltpu.CompilerParams(
            collective_id=0, has_side_effects=True, vmem_limit_bytes=58 * 1024 * 1024
        ),
        name="contrast_back",
    )(image_emb, text_feat, text_proj, pos_index, scale, bias)
    return g_image.astype(F32), g_feat.astype(F32), g_proj.astype(F32)


def solution(mesh):
    return jax.shard_map(
        local,
        mesh=mesh,
        in_specs=(
            P(("blk", "dp"), None),
            P(("blk", "dp"), None),
            P("dp", None),
            P(("blk", "dp"), None),
            P(),
            P(),
        ),
        out_specs=(P(("blk", "dp"), None), P(("blk", "dp"), None), P("dp", None)),
        check_vma=False,
    )
```

time: 105 us -> 99.1 us (0.944)
  local copies, waits for them, and re-layouts: 3.77 us -> 0.01 us
  Pallas kernels: 95.6 us -> 92.8 us
  other arithmetic: 3.06 us -> 4.19 us
    unnamed x8 -> x4, local copies, waits for them, and re-layouts: 3.77 us -> 0.01 us
    pallas_call x1, Pallas kernels: 95.6 us -> 92.8 us  [local(): pl.pallas_call(kernel, out_shape=(jax.ShapeDtypeStruct((ROWS, D), BF), ja...]
    convert_element_type x3, other arithmetic: 3.06 us -> 4.19 us  [local(): return (g_image.astype(F32), g_feat.astype(F32), g_proj.astype(F32))]
where the time goes in v2:
time: 99.1 us; the launch traced here: 98.9 us
  Pallas kernels  92.8 us (94%)
  other arithmetic  4.19 us (4%)
  between operations  1.94 us (2%)
    pallas_call x1, Pallas kernels, local(): pl.pallas_call(kernel, out_shape=(jax.ShapeDtypeStruct((ROWS, D), BF), ja...  92.8 us
    convert_element_type x3, other arithmetic, local(): return (g_image.astype(F32), g_feat.astype(F32), g_proj.astype(F32))  4.19 us

profile of v2, /device:TPU:8, one launch (start us, length us, event | category | flops | bytes accessed | tf_op | source)
XLA Modules:
  0.0 98.9 jit_solution(11075240328873844472)
XLA Ops:
  1.9 92.8 %contrast_back.1 = (bf16[256,1152]{1,0:T(8,128)(2,1)}, bf16[256,1152]{1,0:T(8,128)(2,1)}, bf16[144,1152]{1,0:T(8,128)(2,1)}) custom-call(bf16[256,1152]{1,0:T(8,128)(2,1)} %image_h.1, bf16[256,1152]{1,0:T(8,128)(2,1)} %feat_h.1, bf16[144,1152]{1,0:T(8,128)(2,1)} %proj_h.1, s32[1,256]{1,0:T(1,128)} %pos_h.1, f32[1]{0:T(128)S(6)} %copy.9.scale, f32[1]{0:T(128)S(6)} %copy.10.bias), custom_call_target="tpu_custom_call" | custom-call | tf_op jit(solution)/shard_map/contrast_back/pallas_call | solution.py:482
  94.7 0.0 copy-start
  94.7 2.2 %convert_element_type.10 = f32[256,1152]{1,0:T(8,128)} convert(bf16[256,1152]{1,0:T(8,128)(2,1)} %get-tuple-element.7) | non-fusion elementwise | flops 294912 | bytes 1769472 | tf_op jit(solution)/shard_map/convert_element_type | solution.py:497
  96.9 0.0 copy-start.1
  96.9 0.0 copy-done
  96.9 1.1 %convert_element_type.9 = f32[256,1152]{1,0:T(8,128)} convert(bf16[256,1152]{1,0:T(8,128)(2,1)S(1)} %copy-done) | non-fusion elementwise | flops 294912 | bytes 1769472 | tf_op jit(solution)/shard_map/convert_element_type | solution.py:497
  98.0 0.0 copy-done.1
  98.0 0.9 convert_element_type.11
Async XLA Ops:
  94.7 2.2 %copy-start = (bf16[256,1152]{1,0:T(8,128)(2,1)S(1)}, bf16[256,1152]{1,0:T(8,128)(2,1)}, u32[]{:S(2)}) copy-start(bf16[256,1152]{1,0:T(8,128)(2,1)} %get-tuple-element.6) | copy-start | bytes 1769476
  96.9 1.1 %copy-start.1 = (bf16[144,1152]{1,0:T(8,128)(2,1)S(1)}, bf16[144,1152]{1,0:T(8,128)(2,1)}, u32[]{:S(2)}) copy-start(bf16[144,1152]{1,0:T(8,128)(2,1)} %get-tuple-element.8) | copy-start | bytes 995332

commit v3 on v2

--- a/solution.py
+++ b/solution.py
@@ -84,7 +84,7 @@
     full, image, feat, pos, image_n, feat_p, feat_k, tft, tft_o, unit_in, unit_tp, inv_i, inv_t,
     text, text_p, acc_t, acc_i, coef_o, gte, gte_o, part, send_a, send_b, got_a, got_b,
     mid_a, mid_b, got_a2, got_b2, zin, got_z, fin,
-    hop, s_in, relay, s_fwd, r_hop,
+    hop, hop_t, f_image, f_feat, f_proj, s_in, s_out, relay, s_fwd, r_hop,
     s_img, r_img, s_txt, r_txt, s_py, r_py, s_pt, r_pt, s_px, r_px, s_pc, r_pc,
     s_tf, r_tf, s_ge, r_ge, s_a, r_a, s_b, r_b, s_a2, r_a2, s_b2, r_b2,
     s_z, r_z, s_gz, r_gz, s_gx, r_gx, s_gy, r_gy,
@@ -154,8 +154,11 @@
         copy(cut(hop, i), cut(image_n, direct + i), s_fwd.at[i], r_img.at[direct + i], to_z[NZ - 1])
         for i in range(VIA)
     ]
-    c_txt = copy(feat_h, feat_p, s_txt.at[0], r_txt.at[0], nxt)
-    pending += c_img + [c_txt]
+    half = lambda ref, i: ref.at[pl.ds(i * (ROWS // 2), ROWS // 2)]
+    c_txt = [copy(half(feat_h, i), half(feat_p, i), s_txt.at[i], r_txt.at[i], nxt) for i in range(2)]
+    t_hop = copy(half(feat_h, 1), hop_t, s_txt.at[1], r_hop.at[VIA], to_after)
+    t_fwd = copy(hop_t, half(feat_p, 1), s_fwd.at[VIA], r_txt.at[1], to_z[1])
+    pending += c_img + c_txt
     for i in range(direct):
         c_img[i].start()
 
@@ -192,7 +195,8 @@
 
     @pl.when(z != NZ - 1)
     def _():
-        c_txt.start()
+        for cp in c_txt:
+            cp.start()
 
     for cp in loads:
         cp.wait()
@@ -251,7 +255,8 @@
 
     @pl.when(z == NZ - 1)
     def _():
-        c_txt.start()
+        c_txt[0].start()
+        t_hop.start()
 
     for i in range(IMG):
         c_img[i].wait_recv()
@@ -337,12 +342,19 @@
     b_copy(twin).start()
     pass_on(2)
 
+    @pl.when(z == NZ - 1)
+    def _():
+        t_hop.wait_recv()
+        t_fwd.start()
+
     def feat_cols(i, _):
         cols = pl.ds(pl.multiple_of(i * COLS, COLS), COLS)
-        g_feat[:, cols] = nt_dot(gte[...], full[cols]).astype(BF)
+        f_feat[:, cols] = nt_dot(gte[...], full[cols]).astype(BF)
         return 0
 
     lax.fori_loop(0, D // COLS, feat_cols, 0)
+    out_feat = pltpu.make_async_copy(f_feat, g_feat, s_out.at[0])
+    out_feat.start()
 
     def sum_a(i):
         for o in range(1, NX):
@@ -406,7 +418,8 @@
     own = fin.at[low, x, z]
     c_gz = [send(own, own, s_gz.at[o - 1], r_gz.at[o - 1], to_z[o]) for o in range(1, NZ)]
 
-    c_txt.wait_recv()
+    for cp in c_txt:
+        cp.wait_recv()
 
     def text_p_cols(cols):
         text_p[:, cols] = nn_dot(feat_p[...], full[:, cols])
@@ -420,7 +433,9 @@
         acc_i[:, cols] = nn_dot(coef_both, unit_tp[:, cols])
 
     by_columns(image_cols)
-    norm_back(image, inv_i, acc_i, factor, g_image, 64)
+    norm_back(image, inv_i, acc_i, factor, f_image, 64)
+    out_image = pltpu.make_async_copy(f_image, g_image, s_out.at[1])
+    out_image.start()
 
     for cp in c_gz:
         cp.wait_recv()
@@ -436,7 +451,9 @@
     for t in range(TILES):
         l, xo, u = t // (NX * UN), (t // UN) % NX, t % UN
         row, col = (t // 9) * 16, (t % 9) * 128
-        g_proj[row : row + 16, col : col + 128] = fin[l, xo, u]
+        f_proj[row : row + 16, col : col + 128] = fin[l, xo, u]
+    out_proj = pltpu.make_async_copy(f_proj, g_proj, s_out.at[2])
+    out_proj.start()
     for cp in pending:
         cp.wait_send()
     for i in range(NH):
@@ -450,6 +467,30 @@
     def _():
         for cp in c_fwd:
             cp.wait_send()
+
+    @pl.when(z == NZ - 1)
+    def _():
+        t_fwd.wait_send()
+
+    for cp in (out_feat, out_image, out_proj):
+        cp.wait()
+
+
+def widen(*refs):
+    srcs, dsts, narrow, wide, (s_in, s_out) = refs[:3], refs[3:6], refs[6:9], refs[9:12], refs[12:]
+    pieces = [(a, r, 64) for a in range(2) for r in range(0, ROWS, 64)] + [(2, r, 48) for r in range(0, SH, 48)]
+    ins, outs = [], []
+    for i, (a, r, n) in enumerate(pieces):
+        rows = pl.ds(r, n)
+        ins.append(pltpu.make_async_copy(srcs[a].at[rows], narrow[a].at[rows], s_in.at[i]))
+        outs.append(pltpu.make_async_copy(wide[a].at[rows], dsts[a].at[rows], s_out.at[i]))
+        ins[-1].start()
+    for i, (a, r, n) in enumerate(pieces):
+        ins[i].wait()
+        wide[a][r : r + n] = narrow[a][r : r + n].astype(F32)
+        outs[i].start()
+    for cp in outs:
+        cp.wait()
 
 
 def local(image_emb, text_feat, text_proj, pos_index, scale, bias):
@@ -468,15 +509,16 @@
         vm((NY, UA, 16, 128), BF), vm((NX, UB, 16, 128), BF),
         vm((NY, UA, 16, 128), BF), vm((NX - 1, UB, 16, 128), BF),
         vm((NZ, 16, 128), BF), vm((NZ - 1, 16, 128), BF), vm((2, NX, NZ, 16, 128), BF),
-        vm((VIA * ROWS // IMG, D), BF), pltpu.SemaphoreType.DMA((4,)), pltpu.SemaphoreType.REGULAR((5,)),
-        pltpu.SemaphoreType.DMA((VIA,)), pltpu.SemaphoreType.DMA((VIA,)),
+        vm((VIA * ROWS // IMG, D), BF), vm((ROWS // 2, D), BF),
+        vm((ROWS, D), BF), vm((ROWS, D), BF), vm((SH, D), BF),
+        pltpu.SemaphoreType.DMA((4,)), pltpu.SemaphoreType.DMA((3,)), pltpu.SemaphoreType.REGULAR((5,)),
+        pltpu.SemaphoreType.DMA((VIA + 1,)), pltpu.SemaphoreType.DMA((VIA + 1,)),
     ]
     sems = (
-        dma(IMG) + dma(1) + dma(3) + dma(3) + dma(3, NX - 1) + dma(16) + dma(1) + dma(4)
+        dma(IMG) + dma(2) + dma(3) + dma(3) + dma(3, NX - 1) + dma(16) + dma(1) + dma(4)
         + dma(NX - 1, NH) + dma(NY) + dma(NY) + dma(NX - 1)
         + dma(NZ - 1) + dma(NZ - 1) + dma(NX - 1) + dma(NX)
     )
-    whole = pl.BlockSpec(memory_space=pltpu.VMEM)
     scalar = pl.BlockSpec(memory_space=pltpu.SMEM)
     far = pl.BlockSpec(memory_space=pltpu.HBM)
     g_image, g_feat, g_proj = pl.pallas_call(
@@ -487,14 +529,24 @@
             jax.ShapeDtypeStruct((SH, D), BF),
         ),
         in_specs=[far, far, far, far, scalar, scalar],
-        out_specs=(whole, whole, whole),
+        out_specs=(far, far, far),
         scratch_shapes=scratch + sems,
         compiler_params=pltpu.CompilerParams(
             collective_id=0, has_side_effects=True, vmem_limit_bytes=58 * 1024 * 1024
         ),
         name="contrast_back",
     )(image_emb, text_feat, text_proj, pos_index, scale, bias)
-    return g_image.astype(F32), g_feat.astype(F32), g_proj.astype(F32)
+    sizes = ((ROWS, D), (ROWS, D), (SH, D))
+    return pl.pallas_call(
+        widen,
+        out_shape=tuple(jax.ShapeDtypeStruct(n, F32) for n in sizes),
+        in_specs=[far] * 3,
+        out_specs=(far,) * 3,
+        scratch_shapes=[vm(n, BF) for n in sizes] + [vm(n, F32) for n in sizes]
+        + [pltpu.SemaphoreType.DMA((11,)), pltpu.SemaphoreType.DMA((11,))],
+        compiler_params=pltpu.CompilerParams(vmem_limit_bytes=58 * 1024 * 1024),
+        name="widen",
+    )(g_image, g_feat, g_proj)
 
 
 def solution(mesh):

time: 99.1 us -> 91 us (0.918)
  other arithmetic: 4.19 us -> 0 us
  Pallas kernels: 92.8 us -> 88.9 us
    pallas_call x1, Pallas kernels: 92.8 us -> 86.2 us  [local(): pl.pallas_call(kernel, out_shape=(jax.ShapeDtypeStruct((ROWS, D), BF), ja...]
    convert_element_type x3 -> x0, other arithmetic: 4.19 us -> none  [local(): return (g_image.astype(F32), g_feat.astype(F32), g_proj.astype(F32))]
    pallas_call x0 -> x1, Pallas kernels: none -> 2.73 us  [local(): pl.pallas_call(widen, out_shape=tuple((jax.ShapeDtypeStruct(n, F32) for n...]
where the time goes in v3:
time: 91 us; the launch traced here: 90.9 us
  Pallas kernels  88.9 us (98%)
  between operations  1.93 us (2%)
    pallas_call x1, Pallas kernels, local(): pl.pallas_call(kernel, out_shape=(jax.ShapeDtypeStruct((ROWS, D), BF), ja...  86.2 us
    pallas_call x1, Pallas kernels, local(): pl.pallas_call(widen, out_shape=tuple((jax.ShapeDtypeStruct(n, F32) for n...  2.73 us

profile of v3, /device:TPU:8, one launch (start us, length us, event | category | flops | bytes accessed | tf_op | source)
XLA Modules:
  0.0 90.9 jit_solution(7686881167594601707)
XLA Ops:
  1.9 86.2 %contrast_back.1 = (bf16[256,1152]{1,0:T(8,128)(2,1)}, bf16[256,1152]{1,0:T(8,128)(2,1)}, bf16[144,1152]{1,0:T(8,128)(2,1)}) custom-call(bf16[256,1152]{1,0:T(8,128)(2,1)} %image_h.1, bf16[256,1152]{1,0:T(8,128)(2,1)} %feat_h.1, bf16[144,1152]{1,0:T(8,128)(2,1)} %proj_h.1, s32[1,256]{1,0:T(1,128)} %pos_h.1, f32[1]{0:T(128)S(6)} %copy.9.scale, f32[1]{0:T(128)S(6)} %copy.10.bias), custom_call_target="tpu_custom_call" | custom-call | tf_op jit(solution)/shard_map/contrast_back/pallas_call | solution.py:524
  88.1 2.7 %widen.1 = (f32[256,1152]{1,0:T(8,128)}, f32[256,1152]{1,0:T(8,128)}, f32[144,1152]{1,0:T(8,128)}) custom-call(bf16[256,1152]{1,0:T(8,128)(2,1)} %get-tuple-element.6.refs_0_, bf16[256,1152]{1,0:T(8,128)(2,1)} %get-tuple-element.7.refs_1_, bf16[144,1152]{1,0:T(8,128)(2,1)} %get-tuple-element.8.refs_2_), custom_call_target="tpu_custom_call" | custom-call | tf_op jit(solution)/shard_map/widen/pallas_call | solution.py:540

commit v4 on v3

--- a/solution.py
+++ b/solution.py
@@ -16,7 +16,6 @@
 TILES = 81
 COLS = 384
 IMG = 4
-VIA = 2
 
 
 def place():
@@ -84,8 +83,8 @@
     full, image, feat, pos, image_n, feat_p, feat_k, tft, tft_o, unit_in, unit_tp, inv_i, inv_t,
     text, text_p, acc_t, acc_i, coef_o, gte, gte_o, part, send_a, send_b, got_a, got_b,
     mid_a, mid_b, got_a2, got_b2, zin, got_z, fin,
-    hop, hop_t, f_image, f_feat, f_proj, s_in, s_out, relay, s_fwd, r_hop,
-    s_img, r_img, s_txt, r_txt, s_py, r_py, s_pt, r_pt, s_px, r_px, s_pc, r_pc,
+    hop, hop_t, f_image, f_feat, f_proj, s_in, s_out, relay, joined, s_fwd, r_hop,
+    s_img, r_img, s_txt, r_txt, s_py, r_py, r_pt, s_px, r_px, s_pc, r_pc,
     s_tf, r_tf, s_ge, r_ge, s_a, r_a, s_b, r_b, s_a2, r_a2, s_b2, r_b2,
     s_z, r_z, s_gz, r_gz, s_gx, r_gx, s_gy, r_gy,
 ):
@@ -101,7 +100,6 @@
     to_x = [device(v, y, z, c) for v in xs]
     to_y = [device(x, v, z, c) for v in ys]
     to_z = [device(x, y, v, c) for v in zs]
-    pending = []
     col = x * 2 + low
     before, after = lax.rem(col + 7, 8), lax.rem(col + 1, 8)
     to_before = device(before // 2, 2 * h + lax.rem(before, 2), z, c)
@@ -115,16 +113,28 @@
     def send(src, dst, s, r, dev):
         cp = copy(src, dst, s, r, dev)
         cp.start()
-        pending.append(cp)
         return cp
+
+    def all_sent(like, sem):
+        copy(like, like, sem, sem, mate).wait_send()
+
+    def all_here(like, sem):
+        copy(like, like, sem, sem, mate).wait_recv()
 
     def rows16(start, size):
         return pl.ds(pl.multiple_of(start, 16), size)
 
     barrier = pltpu.get_barrier_semaphore()
-    partners = to_x[1:] + to_y[1:] + [mate, prev, nxt, to_z[1], to_z[NZ - 1], to_before, to_after]
+    first, last = z == 0, z == NZ - 1
+    partners = to_x[1:] + to_y[1:] + [mate, prev, to_z[NZ - 1], to_before, to_after]
     for dev in partners:
         pl.semaphore_signal(barrier, inc=1, device_id=dev, device_id_type=MESH)
+
+    @pl.when(jnp.logical_not(last))
+    def _():
+        for dev in (nxt, to_z[1]):
+            pl.semaphore_signal(barrier, inc=1, device_id=dev, device_id_type=MESH)
+
     mine = d * SH
     loads = [
         pltpu.make_async_copy(a, to, s_in.at[i])
@@ -134,7 +144,18 @@
     ]
     for cp in loads:
         cp.start()
-    pl.semaphore_wait(barrier, len(partners))
+
+    @pl.when(first)
+    def _():
+        pl.semaphore_wait(barrier, len(partners))
+
+    @pl.when(jnp.logical_not(first))
+    def _():
+        pl.semaphore_wait(barrier, len(partners) + 2)
+
+    @pl.when(last)
+    def _():
+        pl.semaphore_signal(joined, inc=1, device_id=to_z[1], device_id_type=MESH)
 
     def pass_on(i):
         if i:
@@ -144,33 +165,24 @@
                 pl.semaphore_signal(relay.at[i], inc=1, device_id=dev, device_id_type=MESH)
 
     step = ROWS // IMG
-    direct = IMG - VIA
     cut = lambda ref, i: ref.at[pl.ds(i * step, step)]
-    c_img = [copy(cut(image_h, i), cut(image_n, i), s_img.at[i], r_img.at[i], prev) for i in range(IMG)]
-    c_hop = [
-        copy(cut(image_h, direct + i), cut(hop, i), s_img.at[direct + i], r_hop.at[i], to_before) for i in range(VIA)
-    ]
-    c_fwd = [
-        copy(cut(hop, i), cut(image_n, direct + i), s_fwd.at[i], r_img.at[direct + i], to_z[NZ - 1])
-        for i in range(VIA)
-    ]
+    c_img = [copy(cut(image_h, i), cut(image_n, i), s_img.at[0], r_img.at[i], prev) for i in range(IMG)]
+    c_hop = [copy(cut(image_h, i), cut(hop, i), s_img.at[0], r_hop.at[i], to_before) for i in range(IMG)]
+    c_fwd = [copy(cut(hop, i), cut(image_n, i), s_fwd.at[0], r_img.at[i], to_z[NZ - 1]) for i in range(IMG)]
     half = lambda ref, i: ref.at[pl.ds(i * (ROWS // 2), ROWS // 2)]
-    c_txt = [copy(half(feat_h, i), half(feat_p, i), s_txt.at[i], r_txt.at[i], nxt) for i in range(2)]
-    t_hop = copy(half(feat_h, 1), hop_t, s_txt.at[1], r_hop.at[VIA], to_after)
-    t_fwd = copy(hop_t, half(feat_p, 1), s_fwd.at[VIA], r_txt.at[1], to_z[1])
-    pending += c_img + c_txt
-    for i in range(direct):
-        c_img[i].start()
-
-    @pl.when(z == 0)
-    def _():
-        for i in range(VIA):
-            c_hop[i].start()
-
-    @pl.when(z != 0)
-    def _():
-        for i in range(VIA):
-            c_img[direct + i].start()
+    c_txt = [copy(half(feat_h, i), half(feat_p, i), s_txt.at[0], r_txt.at[0], nxt) for i in range(2)]
+    t_hop = copy(half(feat_h, 1), hop_t, s_txt.at[0], r_hop.at[IMG], to_after)
+    t_fwd = copy(hop_t, half(feat_p, 1), s_fwd.at[1], r_txt.at[0], to_z[1])
+
+    @pl.when(first)
+    def _():
+        for cp in c_hop:
+            cp.start()
+
+    @pl.when(jnp.logical_not(first))
+    def _():
+        for cp in c_img:
+            cp.start()
 
     sign = 2 * low - 1
     xrow = x * PART
@@ -181,19 +193,19 @@
         c_py.append(
             send(
                 proj_h.at[rows16(xrow, PART)], full.at[rows16(mine + xrow, PART)],
-                s_py.at[k], r_py.at[k], ahead[k],
+                s_py.at[0], r_py.at[k], ahead[k],
             )
         )
-    c_pc = [[], [], [], [send(proj_h, full.at[rows16(mine, SH)], s_pc.at[15], r_pc.at[15], mate)]]
+    send(proj_h, full.at[rows16(mine, SH)], s_pc.at[0], r_pc.at[3], mate)
     for k in range(3):
         c_pt.append(
             send(
                 proj_h.at[pl.ds(NX * PART, rest)], full.at[rows16(mine + NX * PART, rest)],
-                s_pt.at[k], r_pt.at[k], ahead[k],
+                s_py.at[0], r_pt.at[k], ahead[k],
             )
         )
 
-    @pl.when(z != NZ - 1)
+    @pl.when(jnp.logical_not(last))
     def _():
         for cp in c_txt:
             cp.start()
@@ -209,27 +221,33 @@
         feat_k[i] = feat[:, i * 2 * SH : (i + 1) * 2 * SH]
 
     pairs, rows_of = [], []
-    for hop in (1, -2, 3):
-        src_y = lax.rem(y + sign * hop + NY, NY)
+    for way in (1, -2, 3):
+        src_y = lax.rem(y + sign * way + NY, NY)
         pairs.append(src_y // 2)
         rows_of.append(((src_y // 2) * 2 + c) * SH)
 
-    def to_mate(k, i, start, size):
+    def to_mate(k, start, size):
         where = full.at[rows16(start, size)]
-        c_pc[k].append(send(where, where, s_pc.at[k * 5 + i], r_pc.at[k * 5 + i], mate))
-
-    c_px = []
+        send(where, where, s_pc.at[0], r_pc.at[k], mate)
+
+    def mate_sent(k):
+        all_here(full.at[pl.ds(0, SH)], r_pc.at[k])
+
     for k in range(3):
         c_py[k].wait_recv()
         where = full.at[rows16(rows_of[k] + xrow, PART)]
-        c_px.append([send(where, where, s_px.at[k, o - 1], r_px.at[k, o - 1], to_x[o]) for o in range(1, NX)])
-        to_mate(k, 0, rows_of[k] + xrow, PART)
-
-    @pl.when(z == 0)
-    def _():
-        for i in range(VIA):
+        for o in range(1, NX):
+            send(where, where, s_px.at[0], r_px.at[k], to_x[o])
+        to_mate(k, rows_of[k] + xrow, PART)
+
+    @pl.when(first)
+    def _():
+        pl.semaphore_wait(joined, 1)
+        for i in range(IMG):
             c_hop[i].wait_recv()
             c_fwd[i].start()
+
+    pass_on(0)
 
     def add_text(pair, first):
         rhs_rows = rows16(pair * (2 * SH), 2 * SH)
@@ -240,29 +258,28 @@
 
         by_columns(cols_of)
 
-    c_pc[3][0].wait_recv()
+    mate_sent(3)
     add_text(h, True)
     for k in range(3):
+        all_here(full.at[pl.ds(0, (NX - 1) * PART)], r_px.at[k])
         for o in range(1, NX):
-            c_px[k][o - 1].wait_recv()
-            to_mate(k, o, rows_of[k] + lax.rem(x + NX - o, NX) * PART, PART)
+            to_mate(k, rows_of[k] + xs[NX - o] * PART, PART)
         c_pt[k].wait_recv()
-        to_mate(k, 4, rows_of[k] + NX * PART, rest)
+        to_mate(k, rows_of[k] + NX * PART, rest)
         if k:
-            for cp in c_pc[k - 1]:
-                cp.wait_recv()
+            mate_sent(k - 1)
             add_text(pairs[k - 1], False)
 
-    @pl.when(z == NZ - 1)
+    @pl.when(last)
     def _():
         c_txt[0].start()
         t_hop.start()
 
+    pass_on(1)
     for i in range(IMG):
         c_img[i].wait_recv()
         unit_rows(image_n.at[pl.ds(i * step, step)], unit_in.at[pl.ds(ROWS + i * step, step)], None)
-    for cp in c_pc[2]:
-        cp.wait_recv()
+    mate_sent(2)
     add_text(pairs[2], False)
     unit_t = unit_tp.at[pl.ds(0, ROWS)]
     unit_rows(text, unit_t, inv_t)
@@ -280,23 +297,20 @@
         acc_t[:, cols] = nn_dot(coef_all, unit_in[:, cols])
 
     by_columns(text_grads)
-    c_ge = []
 
     def share(i, rows):
-        c_ge.append(send(gte.at[rows], gte_o.at[rows], s_ge.at[i], r_ge.at[i], mate))
+        send(gte.at[rows], gte_o.at[rows], s_ge.at[0], r_ge.at[0], mate)
 
     norm_back(text, inv_t, acc_t, factor, gte, 64, share)
-    pass_on(0)
+    pass_on(2)
     tft_c = tft[c].reshape(NH * SH, ROWS)
 
     def first_half(cols):
         part[:, cols] = nn_dot(tft_c, gte[:, cols])
 
     by_columns(first_half)
-    pass_on(1)
     c_tf.wait_recv()
-    for cp in c_ge:
-        cp.wait_recv()
+    all_here(gte_o, r_ge.at[0])
 
     def group(i):
         return lax.rem(h + 1 + i, NH)
@@ -318,13 +332,13 @@
 
     def a_copy(i, o):
         two = pl.ds(2 * group(i), 2)
-        return copy(send_a.at[xs[o], two], got_a.at[o - 1, two], s_a.at[o - 1, i], r_a.at[o - 1, i], to_x[o])
+        return copy(send_a.at[xs[o], two], got_a.at[o - 1, two], s_a.at[0], r_a.at[i], to_x[o])
 
     def b_copy(to):
-        return copy(send_b.at[to], got_b.at[y], s_b.at[to], r_b.at[y], device(x, to, z, c))
+        return copy(send_b.at[to], got_b.at[y], s_b.at[0], r_b.at[0], device(x, to, z, c))
 
     def a2_copy(to):
-        return copy(mid_a.at[to], got_a2.at[y], s_a2.at[to], r_a2.at[y], device(x, to, z, c))
+        return copy(mid_a.at[to], got_a2.at[y], s_a2.at[0], r_a2.at[0], device(x, to, z, c))
 
     def start_group(i, _):
         second_half(i)
@@ -340,9 +354,10 @@
     for o in range(1, NX):
         a_copy(NH - 1, o).start()
     b_copy(twin).start()
-    pass_on(2)
-
-    @pl.when(z == NZ - 1)
+
+    pass_on(3)
+
+    @pl.when(last)
     def _():
         t_hop.wait_recv()
         t_fwd.start()
@@ -357,8 +372,7 @@
     out_feat.start()
 
     def sum_a(i):
-        for o in range(1, NX):
-            a_copy(i, o).wait_recv()
+        all_here(got_a.at[:, pl.ds(2 * group(i), 2)], r_a.at[i])
         for l in range(2):
             at = 2 * group(i) + l
             v = send_a[x, at].astype(F32)
@@ -372,17 +386,12 @@
             a2_copy(2 * group(i) + l).start()
         return 0
 
-    pass_on(3)
+    pass_on(4)
     lax.fori_loop(0, NH - 1, a_group, 0)
     sum_a(NH - 1)
     a2_copy(twin).start()
-    pass_on(4)
-
-    def received(sem, slots, at):
-        copy(slots.at[at], slots.at[at], sem.at[at], sem.at[at], mate).wait_recv()
-
-    for o in range(1, NY):
-        received(r_b, got_b, ys[o])
+
+    all_here(got_b.at[pl.ds(0, NY - 1)], r_b.at[0])
 
     def sum_b(i, _):
         v = send_b[y, i].astype(F32)
@@ -392,16 +401,15 @@
         return 0
 
     lax.fori_loop(0, NX, sum_b, 0)
-    c_b2 = [send(mid_b.at[xs[o]], got_b2.at[o - 1], s_b2.at[o - 1], r_b2.at[o - 1], to_x[o]) for o in range(1, NX)]
-
-    for o in range(1, NY):
-        received(r_a2, got_a2, ys[o])
+    for o in range(1, NX):
+        send(mid_b.at[xs[o]], got_b2.at[o - 1], s_b2.at[0], r_b2.at[0], to_x[o])
+
+    all_here(got_a2.at[pl.ds(0, NY - 1)], r_a2.at[0])
     v = mid_a[y].astype(F32)
     for o in range(1, NY):
         v = v + got_a2[ys[o]].astype(F32)
     zin[0:UA] = v.astype(BF)
-    for cp in c_b2:
-        cp.wait_recv()
+    all_here(got_b2, r_b2.at[0])
     v = mid_b[x].astype(F32)
     for o in range(NX - 1):
         v = v + got_b2[o].astype(F32)
@@ -409,17 +417,18 @@
     zin[UN] = jnp.zeros((16, 128), BF)
 
     pass_on(5)
-    c_z = [send(zin.at[zs[o]], got_z.at[o - 1], s_z.at[o - 1], r_z.at[o - 1], to_z[o]) for o in range(1, NZ)]
+    for o in range(1, NZ):
+        send(zin.at[zs[o]], got_z.at[o - 1], s_z.at[0], r_z.at[0], to_z[o])
+    all_here(got_z, r_z.at[0])
     v = zin[z].astype(F32)
     for o in range(NZ - 1):
-        c_z[o].wait_recv()
         v = v + got_z[o].astype(F32)
     fin[low, x, z] = v.astype(BF)
     own = fin.at[low, x, z]
-    c_gz = [send(own, own, s_gz.at[o - 1], r_gz.at[o - 1], to_z[o]) for o in range(1, NZ)]
-
-    for cp in c_txt:
-        cp.wait_recv()
+    for o in range(1, NZ):
+        send(own, own, s_gz.at[0], r_gz.at[0], to_z[o])
+
+    all_here(feat_p, r_txt.at[0])
 
     def text_p_cols(cols):
         text_p[:, cols] = nn_dot(feat_p[...], full[:, cols])
@@ -437,38 +446,35 @@
     out_image = pltpu.make_async_copy(f_image, g_image, s_out.at[1])
     out_image.start()
 
-    for cp in c_gz:
-        cp.wait_recv()
+    all_here(got_z, r_gz.at[0])
     own = fin.at[low, x, pl.ds(0, UN)]
-    c_gy = [send(own, own, s_gy.at[0], r_gy.at[0], device(x, twin, z, c))]
-    c_gx = [send(own, own, s_gx.at[o - 1], r_gx.at[o - 1], to_x[o]) for o in range(1, NX)]
+    send(own, own, s_gy.at[0], r_gy.at[0], device(x, twin, z, c))
+    c_gx = [send(own, own, s_gx.at[0], r_gx.at[o - 1], to_x[o]) for o in range(1, NX)]
     for o in (1, 3, 2):
         c_gx[o - 1].wait_recv()
         got = fin.at[low, xs[NX - o], pl.ds(0, UN)]
-        c_gy.append(send(got, got, s_gy.at[o], r_gy.at[o], device(x, twin, z, c)))
-    for cp in c_gy:
-        cp.wait_recv()
+        send(got, got, s_gy.at[0], r_gy.at[0], device(x, twin, z, c))
+    block = fin.at[low, :, pl.ds(0, UN)]
+    all_here(block, r_gy.at[0])
     for t in range(TILES):
         l, xo, u = t // (NX * UN), (t // UN) % NX, t % UN
         row, col = (t // 9) * 16, (t % 9) * 128
         f_proj[row : row + 16, col : col + 128] = fin[l, xo, u]
     out_proj = pltpu.make_async_copy(f_proj, g_proj, s_out.at[2])
     out_proj.start()
-    for cp in pending:
-        cp.wait_send()
-    for i in range(NH):
-        for o in range(1, NX):
-            a_copy(i, o).wait_send()
-    for o in range(1, NY):
-        b_copy(ys[o]).wait_send()
-        a2_copy(ys[o]).wait_send()
-
-    @pl.when(z == 0)
-    def _():
-        for cp in c_fwd:
-            cp.wait_send()
-
-    @pl.when(z == NZ - 1)
+    for like, sem in (
+        (image, s_img), (feat, s_txt), (full.at[pl.ds(0, SH)], s_py), (tft_o, s_tf), (gte_o, s_ge),
+        (full.at[pl.ds(0, 3 * (NX - 1) * PART)], s_px), (full.at[pl.ds(0, NH * SH)], s_pc),
+        (got_a, s_a), (got_b.at[pl.ds(0, NY - 1)], s_b), (got_a2.at[pl.ds(0, NY - 1)], s_a2), (got_b2, s_b2),
+        (got_z, s_z), (got_z, s_gz), (fin.at[low, pl.ds(0, NX - 1), pl.ds(0, UN)], s_gx), (block, s_gy),
+    ):
+        all_sent(like, sem.at[0])
+
+    @pl.when(first)
+    def _():
+        all_sent(hop, s_fwd.at[0])
+
+    @pl.when(last)
     def _():
         t_fwd.wait_send()
 
@@ -494,7 +500,7 @@
 
 
 def local(image_emb, text_feat, text_proj, pos_index, scale, bias):
-    dma = lambda *shape: [pltpu.SemaphoreType.DMA(shape), pltpu.SemaphoreType.DMA(shape)]
+    dma = lambda *into: sum(([pltpu.SemaphoreType.DMA((n,))] for n in (1,) + into), [])
     vm = pltpu.VMEM
     scratch = [
         vm((D, D), BF), vm((ROWS, D), BF), vm((ROWS, D), BF), vm((1, ROWS), jnp.int32),
@@ -509,15 +515,14 @@
         vm((NY, UA, 16, 128), BF), vm((NX, UB, 16, 128), BF),
         vm((NY, UA, 16, 128), BF), vm((NX - 1, UB, 16, 128), BF),
         vm((NZ, 16, 128), BF), vm((NZ - 1, 16, 128), BF), vm((2, NX, NZ, 16, 128), BF),
-        vm((VIA * ROWS // IMG, D), BF), vm((ROWS // 2, D), BF),
-        vm((ROWS, D), BF), vm((ROWS, D), BF), vm((SH, D), BF),
-        pltpu.SemaphoreType.DMA((4,)), pltpu.SemaphoreType.DMA((3,)), pltpu.SemaphoreType.REGULAR((5,)),
-        pltpu.SemaphoreType.DMA((VIA + 1,)), pltpu.SemaphoreType.DMA((VIA + 1,)),
+        vm((ROWS, D), BF),
+        vm((ROWS // 2, D), BF), vm((ROWS, D), BF), vm((ROWS, D), BF), vm((SH, D), BF),
+        pltpu.SemaphoreType.DMA((4,)), pltpu.SemaphoreType.DMA((3,)), pltpu.SemaphoreType.REGULAR((5,)), pltpu.SemaphoreType.REGULAR,
+        pltpu.SemaphoreType.DMA((2,)), pltpu.SemaphoreType.DMA((IMG + 1,)),
     ]
     sems = (
-        dma(IMG) + dma(2) + dma(3) + dma(3) + dma(3, NX - 1) + dma(16) + dma(1) + dma(4)
-        + dma(NX - 1, NH) + dma(NY) + dma(NY) + dma(NX - 1)
-        + dma(NZ - 1) + dma(NZ - 1) + dma(NX - 1) + dma(NX)
+        dma(IMG) + dma(1) + dma(3, 3) + dma(3) + dma(4) + dma(1) + dma(1)
+        + dma(NH) + dma(1) + dma(1) + dma(1) + dma(1) + dma(1) + dma(NX - 1) + dma(1)
     )
     scalar = pl.BlockSpec(memory_space=pltpu.SMEM)
     far = pl.BlockSpec(memory_space=pltpu.HBM)

time: 91 us -> 84.6 us (0.930)
  Pallas kernels: 88.9 us -> 82.4 us
    pallas_call x1, Pallas kernels: 86.2 us -> 79.7 us  [local(): pl.pallas_call(kernel, out_shape=(jax.ShapeDtypeStruct((ROWS, D), BF), ja...]
where the time goes in v4:
time: 84.6 us; the launch traced here: 84.4 us
  Pallas kernels  82.4 us (97%)
  between operations  1.93 us (2%)
    pallas_call x1, Pallas kernels, local(): pl.pallas_call(kernel, out_shape=(jax.ShapeDtypeStruct((ROWS, D), BF), ja...  79.7 us
    pallas_call x1, Pallas kernels, local(): pl.pallas_call(widen, out_shape=tuple((jax.ShapeDtypeStruct(n, F32) for n...  2.73 us

profile of v4, /device:TPU:8, one launch (start us, length us, event | category | flops | bytes accessed | tf_op | source)
XLA Modules:
  0.0 84.4 jit_solution(14870527403203881003)
XLA Ops:
  1.9 79.7 %contrast_back.1 = (bf16[256,1152]{1,0:T(8,128)(2,1)}, bf16[256,1152]{1,0:T(8,128)(2,1)}, bf16[144,1152]{1,0:T(8,128)(2,1)}) custom-call(bf16[256,1152]{1,0:T(8,128)(2,1)} %image_h.1, bf16[256,1152]{1,0:T(8,128)(2,1)} %feat_h.1, bf16[144,1152]{1,0:T(8,128)(2,1)} %proj_h.1, s32[1,256]{1,0:T(1,128)} %pos_h.1, f32[1]{0:T(128)S(6)} %copy.9.scale, f32[1]{0:T(128)S(6)} %copy.10.bias), custom_call_target="tpu_custom_call" | custom-call | tf_op jit(solution)/shard_map/contrast_back/pallas_call | solution.py:529
  81.6 2.7 %widen.1 = (f32[256,1152]{1,0:T(8,128)}, f32[256,1152]{1,0:T(8,128)}, f32[144,1152]{1,0:T(8,128)}) custom-call(bf16[256,1152]{1,0:T(8,128)(2,1)} %get-tuple-element.6.refs_0_, bf16[256,1152]{1,0:T(8,128)(2,1)} %get-tuple-element.7.refs_1_, bf16[144,1152]{1,0:T(8,128)(2,1)} %get-tuple-element.8.refs_2_), custom_call_target="tpu_custom_call" | custom-call | tf_op jit(solution)/shard_map/widen/pallas_call | solution.py:545

commit v5 on v4

--- a/solution.py
+++ b/solution.py
@@ -83,7 +83,7 @@
     full, image, feat, pos, image_n, feat_p, feat_k, tft, tft_o, unit_in, unit_tp, inv_i, inv_t,
     text, text_p, acc_t, acc_i, coef_o, gte, gte_o, part, send_a, send_b, got_a, got_b,
     mid_a, mid_b, got_a2, got_b2, zin, got_z, fin,
-    hop, hop_t, f_image, f_feat, f_proj, s_in, s_out, relay, joined, s_fwd, r_hop,
+    hop, hop_t, f_image, f_feat, s_in, s_out, relay, joined, s_fwd, r_hop,
     s_img, r_img, s_txt, r_txt, s_py, r_py, r_pt, s_px, r_px, s_pc, r_pc,
     s_tf, r_tf, s_ge, r_ge, s_a, r_a, s_b, r_b, s_a2, r_a2, s_b2, r_b2,
     s_z, r_z, s_gz, r_gz, s_gx, r_gx, s_gy, r_gy,
@@ -448,20 +448,17 @@
 
     all_here(got_z, r_gz.at[0])
     own = fin.at[low, x, pl.ds(0, UN)]
-    send(own, own, s_gy.at[0], r_gy.at[0], device(x, twin, z, c))
+    to_twin = device(x, twin, z, c)
+    send(own, g_proj.at[low, x, pl.ds(0, UN)], s_gy.at[0], r_gy.at[0], to_twin)
     c_gx = [send(own, own, s_gx.at[0], r_gx.at[o - 1], to_x[o]) for o in range(1, NX)]
     for o in (1, 3, 2):
         c_gx[o - 1].wait_recv()
-        got = fin.at[low, xs[NX - o], pl.ds(0, UN)]
-        send(got, got, s_gy.at[0], r_gy.at[0], device(x, twin, z, c))
+        at = xs[NX - o]
+        send(fin.at[low, at, pl.ds(0, UN)], g_proj.at[low, at, pl.ds(0, UN)], s_gy.at[0], r_gy.at[0], to_twin)
     block = fin.at[low, :, pl.ds(0, UN)]
+    out_proj = pltpu.make_async_copy(block, g_proj.at[low, :, pl.ds(0, UN)], s_out.at[2])
+    out_proj.start()
     all_here(block, r_gy.at[0])
-    for t in range(TILES):
-        l, xo, u = t // (NX * UN), (t // UN) % NX, t % UN
-        row, col = (t // 9) * 16, (t % 9) * 128
-        f_proj[row : row + 16, col : col + 128] = fin[l, xo, u]
-    out_proj = pltpu.make_async_copy(f_proj, g_proj, s_out.at[2])
-    out_proj.start()
     for like, sem in (
         (image, s_img), (feat, s_txt), (full.at[pl.ds(0, SH)], s_py), (tft_o, s_tf), (gte_o, s_ge),
         (full.at[pl.ds(0, 3 * (NX - 1) * PART)], s_px), (full.at[pl.ds(0, NH * SH)], s_pc),
@@ -482,19 +479,28 @@
         cp.wait()
 
 
-def widen(*refs):
-    srcs, dsts, narrow, wide, (s_in, s_out) = refs[:3], refs[3:6], refs[6:9], refs[9:12], refs[12:]
-    pieces = [(a, r, 64) for a in range(2) for r in range(0, ROWS, 64)] + [(2, r, 48) for r in range(0, SH, 48)]
-    ins, outs = [], []
-    for i, (a, r, n) in enumerate(pieces):
-        rows = pl.ds(r, n)
-        ins.append(pltpu.make_async_copy(srcs[a].at[rows], narrow[a].at[rows], s_in.at[i]))
-        outs.append(pltpu.make_async_copy(wide[a].at[rows], dsts[a].at[rows], s_out.at[i]))
-        ins[-1].start()
-    for i, (a, r, n) in enumerate(pieces):
+def widen(image, feat, tiles, g_image, g_feat, g_proj, n_image, n_feat, n_tiles, w_image, w_feat, w_proj, s_in, s_out):
+    half = ROWS // 2
+    get = lambda src, dst, i: pltpu.make_async_copy(src, dst, s_in.at[i])
+    put = lambda src, dst, i: pltpu.make_async_copy(src, dst, s_out.at[i])
+    pieces = [(a, pl.ds(r, half)) for a in range(2) for r in (0, half)]
+    bf16, f32 = (n_image, n_feat), (w_image, w_feat)
+    ins = [get((image, feat)[a].at[r], bf16[a].at[r], i) for i, (a, r) in enumerate(pieces)]
+    outs = [put(f32[a].at[r], (g_image, g_feat)[a].at[r], i) for i, (a, r) in enumerate(pieces)]
+    ins.append(get(tiles, n_tiles, 4))
+    outs.append(put(w_proj, g_proj, 4))
+    for cp in ins:
+        cp.start()
+    for i, (a, r) in enumerate(pieces):
         ins[i].wait()
-        wide[a][r : r + n] = narrow[a][r : r + n].astype(F32)
+        f32[a][r] = bf16[a][r].astype(F32)
         outs[i].start()
+    ins[4].wait()
+    for t in range(TILES):
+        l, xo, u = t // (NX * UN), (t // UN) % NX, t % UN
+        row, col = (t // 9) * 16, (t % 9) * 128
+        w_proj[row : row + 16, col : col + 128] = n_tiles[l, xo, u].astype(F32)
+    outs[4].start()
     for cp in outs:
         cp.wait()
 
@@ -516,7 +522,7 @@
         vm((NY, UA, 16, 128), BF), vm((NX - 1, UB, 16, 128), BF),
         vm((NZ, 16, 128), BF), vm((NZ - 1, 16, 128), BF), vm((2, NX, NZ, 16, 128), BF),
         vm((ROWS, D), BF),
-        vm((ROWS // 2, D), BF), vm((ROWS, D), BF), vm((ROWS, D), BF), vm((SH, D), BF),
+        vm((ROWS // 2, D), BF), vm((ROWS, D), BF), vm((ROWS, D), BF),
         pltpu.SemaphoreType.DMA((4,)), pltpu.SemaphoreType.DMA((3,)), pltpu.SemaphoreType.REGULAR((5,)), pltpu.SemaphoreType.REGULAR,
         pltpu.SemaphoreType.DMA((2,)), pltpu.SemaphoreType.DMA((IMG + 1,)),
     ]
@@ -531,7 +537,7 @@
         out_shape=(
             jax.ShapeDtypeStruct((ROWS, D), BF),
             jax.ShapeDtypeStruct((ROWS, D), BF),
-            jax.ShapeDtypeStruct((SH, D), BF),
+            jax.ShapeDtypeStruct((2, NX, NZ, 16, 128), BF),
         ),
         in_specs=[far, far, far, far, scalar, scalar],
         out_specs=(far, far, far),
@@ -547,8 +553,8 @@
         out_shape=tuple(jax.ShapeDtypeStruct(n, F32) for n in sizes),
         in_specs=[far] * 3,
         out_specs=(far,) * 3,
-        scratch_shapes=[vm(n, BF) for n in sizes] + [vm(n, F32) for n in sizes]
-        + [pltpu.SemaphoreType.DMA((11,)), pltpu.SemaphoreType.DMA((11,))],
+        scratch_shapes=[vm(g.shape, BF) for g in (g_image, g_feat, g_proj)] + [vm(n, F32) for n in sizes]
+        + [pltpu.SemaphoreType.DMA((5,)), pltpu.SemaphoreType.DMA((5,))],
         compiler_params=pltpu.CompilerParams(vmem_limit_bytes=58 * 1024 * 1024),
         name="widen",
     )(g_image, g_feat, g_proj)

time: 84.6 us -> 83.9 us (level)
  no operation moved by 1% of the time
where the time goes in v5:
time: 83.9 us; the launch traced here: 83.7 us
  Pallas kernels  81.7 us (97%)
  between operations  1.93 us (2%)
    pallas_call x1, Pallas kernels, local(): pl.pallas_call(kernel, out_shape=(jax.ShapeDtypeStruct((ROWS, D), BF), ja...  79 us
    pallas_call x1, Pallas kernels, local(): pl.pallas_call(widen, out_shape=tuple((jax.ShapeDtypeStruct(n, F32) for n...  2.7 us

profile of v5, /device:TPU:8, one launch (start us, length us, event | category | flops | bytes accessed | tf_op | source)
XLA Modules:
  0.0 83.7 jit_solution(17343054944193595201)
XLA Ops:
  1.9 79.0 %contrast_back.1 = (bf16[256,1152]{1,0:T(8,128)(2,1)}, bf16[256,1152]{1,0:T(8,128)(2,1)}, bf16[2,4,12,16,128]{4,3,2,1,0:T(8,128)(2,1)}) custom-call(bf16[256,1152]{1,0:T(8,128)(2,1)} %image_h.1, bf16[256,1152]{1,0:T(8,128)(2,1)} %feat_h.1, bf16[144,1152]{1,0:T(8,128)(2,1)} %proj_h.1, s32[1,256]{1,0:T(1,128)} %pos_h.1, f32[1]{0:T(128)S(6)} %copy.9.scale, ...), custom_call_target="tpu_custom_call" | custom-call | tf_op jit(solution)/shard_map/contrast_back/pallas_call | solution.py:535
  81.0 2.7 %widen.1 = (f32[256,1152]{1,0:T(8,128)}, f32[256,1152]{1,0:T(8,128)}, f32[144,1152]{1,0:T(8,128)}) custom-call(bf16[256,1152]{1,0:T(8,128)(2,1)} %get-tuple-element.6.image, bf16[256,1152]{1,0:T(8,128)(2,1)} %get-tuple-element.7.feat, bf16[2,4,12,16,128]{4,3,2,1,0:T(8,128)(2,1)} %get-tuple-element.8.tiles), custom_call_target="tpu_custom_call" | custom-call | tf_op jit(solution)/shard_map/widen/pallas_call | solution.py:551

commit v6 on v5

--- a/solution.py
+++ b/solution.py
@@ -126,7 +126,7 @@
 
     barrier = pltpu.get_barrier_semaphore()
     first, last = z == 0, z == NZ - 1
-    partners = to_x[1:] + to_y[1:] + [mate, prev, to_z[NZ - 1], to_before, to_after]
+    partners = [to_y[o] for o in (4, 3, 5, 2, 6, 1, 7)] + [to_x[o] for o in (2, 1, 3)] + [mate, prev, to_z[NZ - 1], to_before, to_after]
     for dev in partners:
         pl.semaphore_signal(barrier, inc=1, device_id=dev, device_id_type=MESH)
 
@@ -417,7 +417,8 @@
     zin[UN] = jnp.zeros((16, 128), BF)
 
     pass_on(5)
-    for o in range(1, NZ):
+    far_first = sorted(range(1, NZ), key=lambda o: -min(o, NZ - o))
+    for o in far_first:
         send(zin.at[zs[o]], got_z.at[o - 1], s_z.at[0], r_z.at[0], to_z[o])
     all_here(got_z, r_z.at[0])
     v = zin[z].astype(F32)
@@ -425,7 +426,7 @@
         v = v + got_z[o].astype(F32)
     fin[low, x, z] = v.astype(BF)
     own = fin.at[low, x, z]
-    for o in range(1, NZ):
+    for o in far_first:
         send(own, own, s_gz.at[0], r_gz.at[0], to_z[o])
 
     all_here(feat_p, r_txt.at[0])

time: 83.9 us -> 82.8 us (0.987)
  the two profiles are of different devices: /device:TPU:8 before, /device:TPU:2 now
where the time goes in v6:
time: 82.8 us; the launch traced here: 82.6 us
  Pallas kernels  80.6 us (97%)
  between operations  1.93 us (2%)
    pallas_call x1, Pallas kernels, local(): pl.pallas_call(kernel, out_shape=(jax.ShapeDtypeStruct((ROWS, D), BF), ja...  77.9 us
    pallas_call x1, Pallas kernels, local(): pl.pallas_call(widen, out_shape=tuple((jax.ShapeDtypeStruct(n, F32) for n...  2.7 us

profile of v6, /device:TPU:2, one launch (start us, length us, event | category | flops | bytes accessed | tf_op | source)
XLA Modules:
  0.0 82.6 jit_solution(18401885833277187660)
XLA Ops:
  1.9 77.9 %contrast_back.1 = (bf16[256,1152]{1,0:T(8,128)(2,1)}, bf16[256,1152]{1,0:T(8,128)(2,1)}, bf16[2,4,12,16,128]{4,3,2,1,0:T(8,128)(2,1)}) custom-call(bf16[256,1152]{1,0:T(8,128)(2,1)} %image_h.1, bf16[256,1152]{1,0:T(8,128)(2,1)} %feat_h.1, bf16[144,1152]{1,0:T(8,128)(2,1)} %proj_h.1, s32[1,256]{1,0:T(1,128)} %pos_h.1, f32[1]{0:T(128)S(6)} %copy.9.scale, ...), custom_call_target="tpu_custom_call" | custom-call | tf_op jit(solution)/shard_map/contrast_back/pallas_call | solution.py:536
  79.9 2.7 %widen.1 = (f32[256,1152]{1,0:T(8,128)}, f32[256,1152]{1,0:T(8,128)}, f32[144,1152]{1,0:T(8,128)}) custom-call(bf16[256,1152]{1,0:T(8,128)(2,1)} %get-tuple-element.6.image, bf16[256,1152]{1,0:T(8,128)(2,1)} %get-tuple-element.7.feat, bf16[2,4,12,16,128]{4,3,2,1,0:T(8,128)(2,1)} %get-tuple-element.8.tiles), custom_call_target="tpu_custom_call" | custom-call | tf_op jit(solution)/shard_map/widen/pallas_call | solution.py:552
